TPU v7x, 256 devices: a whole 4x4x8 slice. The times are simulated.
256 devices in a mesh: row: 32 (over z_hi, x, y), col: 8 (over z_lo, core).
Axes of the slice: x: 4, y: 4, z: 8 (z_hi: 2, z_lo: 4; z = z_hi * 4 + z_lo), core: 2. Of those that a mesh axis runs over, the one named last changes fastest.
Arguments:
- features: bfloat16 [256, 32, 64, 128], P('row', None, 'col'), may hold values from -6 to 6
- down_weight: bfloat16 [4, 4, 4, 32, 512], replicated, may hold values from -0.25 to 0.25
- bott_weight: bfloat16 [3, 3, 3, 512, 512], P(None, None, None, 'row'), may hold values from -0.078125 to 0.078125
- up_weight: bfloat16 [4, 4, 4, 32, 512], replicated, may hold values from -0.375 to 0.375
- dec_weight: bfloat16 [3, 3, 3, 32, 32], replicated, may hold values from -0.21875 to 0.21875
Outputs:
- decoded: bfloat16 [256, 32, 64, 128], P('row', None, 'col')
All inputs are finite; a program needn't handle non-finite values.
Results may differ from a plain program's by a relative error of at most 0.015.
Values may be sent and summed in bfloat16 or wider, within the bound.
A program may use at most 128 MiB of HBM per device.

v0:
```python
import jax
import jax.numpy as jnp
from jax import lax
from jax.sharding import PartitionSpec as P


def with_halo(block, sides, width):
    for axis, dim in sides:
        count = lax.axis_size(axis)
        forward = [(i, i + 1) for i in range(count - 1)]
        backward = [(target, source) for source, target in forward]
        low = lax.ppermute(
            lax.slice_in_dim(block, block.shape[dim] - width, None, axis=dim), axis, forward
        )
        high = lax.ppermute(lax.slice_in_dim(block, 0, width, axis=dim), axis, backward)
        block = jnp.concatenate([low, block, high], axis=dim)
    return block


def split_up(shard, dim, size):
    before, after = (shard.shape[:dim], shard.shape[dim + 1 :])
    return jnp.moveaxis(shard.reshape(*before, size, -1, *after), dim, 0)


def sent_and_summed(shard, axis, dim):
    tiles = split_up(shard, dim, lax.axis_size(axis))
    arrived = lax.all_to_all(tiles, axis, split_axis=0, concat_axis=0, tiled=True)
    return arrived.astype(jnp.float32).sum(axis=0)


def convolve(padded, kernel):
    return lax.conv_general_dilated(
        padded[None],
        kernel,
        (1, 1, 1),
        ((0, 0), (0, 0), (1, 1)),
        dimension_numbers=("NDCHW", "DHWIO", "NDCHW"),
        preferred_element_type=jnp.float32,
    )[0]


def body(features, down_weight, bott_weight, up_weight, dec_weight):
    depth, chans, height, width = features.shape
    pooled = (
        features.astype(jnp.float32)
        .reshape(depth // 2, 2, chans, height // 2, 2, width // 2, 2)
        .mean(axis=(1, 4, 6))
        .astype(jnp.bfloat16)
    )
    blocks = pooled.reshape(depth // 8, 4, chans, height // 8, 4, width // 8, 4)
    lowered = jax.nn.silu(
        jnp.einsum("daihbwc,abcio->dohw", blocks, down_weight, preferred_element_type=jnp.float32)
    ).astype(jnp.bfloat16)
    regrouped = lax.all_to_all(lowered, "row", split_axis=1, concat_axis=0, tiled=True)
    rimmed = with_halo(regrouped, (("col", 2),), 1)
    deeper = jnp.pad(rimmed, ((1, 1), (0, 0), (0, 0), (0, 0)))
    summed = sent_and_summed(convolve(deeper, bott_weight).astype(jnp.bfloat16), "row", 0)
    middle = jax.nn.silu(summed).astype(jnp.bfloat16)
    raised = jnp.einsum(
        "dihw,abcoi->daohbwc", middle, up_weight, preferred_element_type=jnp.float32
    )
    raised = raised.reshape(depth // 2, chans, height // 2, width // 2)
    raised = jnp.repeat(jnp.repeat(jnp.repeat(raised, 2, axis=0), 2, axis=2), 2, axis=3)
    joined = (features.astype(jnp.float32) + raised).astype(jnp.bfloat16)
    rimmed_joined = with_halo(joined, (("row", 0), ("col", 2)), 1)
    return jax.nn.silu(convolve(rimmed_joined, dec_weight)).astype(jnp.bfloat16)


def solution(mesh):
    placed = (P("row", None, "col", None), P(), P(None, None, None, "row", None), P(), P())
    return jax.shard_map(
        body, mesh=mesh, in_specs=placed, out_specs=P("row", None, "col", None), check_vma=False
    )
```

profile of v0, /device:TPU:63, one launch (start us, length us, event | category | flops | bytes accessed | tf_op | source)
XLA Modules:
  0.0 154.8 jit_solution(11641234615229443418)
XLA Ops:
  0.0 3.5 %copy.62 = bf16[8,32,8,128]{1,2,3,0:T(8,128)(2,1)} copy(bf16[8,32,8,128]{3,2,1,0:T(8,128)(2,1)} %param.5) | data formatting | bytes 1048576 | tf_op args[0]
  3.5 4.1 %copy.63 = f32[8,32,8,128]{1,3,2,0:T(8,128)} copy(bf16[8,32,8,128]{1,2,3,0:T(8,128)(2,1)} %copy.62) | data formatting | bytes 1572864 | tf_op jit(solution)/shard_map/convert_element_type | solution.py:64
  7.6 4.8 %reduce_sum.18 = f32[4,32,4,64]{1,3,2,0:T(8,128)S(1)} reduce(f32[4,2,32,4,2,64,2]{2,6,5,4,3,1,0:T(2,128)} %bitcast.78, f32[]{:T(128)} %constant.10.clone.1), dimensions={1,4,6}, to_apply=%region_0.0 | reduce | flops 229376 | bytes 1179652 | tf_op jit(solution)/shard_map/reduce_sum | solution.py:47
  12.5 2.3 %fusion.33 = bf16[1,512,1,16]{1,3,2,0:T(8,128)(2,1)S(1)} fusion(bf16[4,4,4,32,512]{4,3,2,1,0:T(8,128)(2,1)} %param.6, bf16[4,32,4,16,4]{1,4,3,2,0:T(4,128)(2,1)S(1)} %bitcast.85), kind=kOutput, calls=%fused_computation.45 | convolution fusion | flops 33595392 | bytes 2179072 | tf_op jit(solution)/shard_map/daihbwc,abcio->dohw/dot_general | solution.py:52
  17.1 20.2 %all_to_all.17 = bf16[32,2,128]{2,1,0:T(2,128)(2,1)S(1)} all-to-all(bf16[32,2,128]{2,1,0:T(2,128)(2,1)S(1)} %reshape.92), channel_id=1, replica_groups=mesh['row'=32,'col'=8] {'row'}, dimensions={0} | all-to-all | bytes 32768 | tf_op jit(solution)/shard_map/all_to_all | solution.py:54
  37.8 4.0 %collective-permute-start.1 = (bf16[32,16,1,16]{1,0,3,2:T(8,128)(2,1)S(1)}, bf16[32,16,1,16]{1,0,3,2:T(8,128)(2,1)S(1)}, u32[]{:S(2)}, u32[]{:S(2)}) collective-permute-start(bf16[32,16,1,16]{1,0,3,2:T(8,128)(2,1)S(1)} %all_to_all.13), channel_id=1, source_target_pairs={{1,0},{2,1},{3,2},{4,3},{5,4},{6,5},{7,6},{9,8},{10,9},{11,10},{12... | collective-permute-start | bytes 49160 | tf_op jit(solution)/shard_map/ppermute | solution.py:15
  41.8 2.5 %collective-permute-start = (bf16[32,16,1,16]{1,0,3,2:T(8,128)(2,1)S(1)}, bf16[32,16,1,16]{1,0,3,2:T(8,128)(2,1)S(1)}, u32[]{:S(2)}, u32[]{:S(2)}) collective-permute-start(bf16[32,16,1,16]{1,0,3,2:T(8,128)(2,1)S(1)} %all_to_all.13), channel_id=1, source_target_pairs={{0,1},{1,2},{2,3},{3,4},{4,5},{5,6},{6,7},{8,9},{9,10},{10,11},{11... | collective-permute-start | bytes 49160 | tf_op jit(solution)/shard_map/ppermute | solution.py:12
  47.6 2.1 %select_convert_fusion = bf16[32,1,8,3,512]{4,2,3,1,0:T(8,128)(2,1)S(1)} fusion(bf16[3,3,3,16,512]{4,3,2,1,0:T(8,128)(2,1)} %param.7, bf16[34,16,3,1,7,2]{1,4,5,2,0,3:T(8,128)(2,1)S(1)} %slice.20, bf16[34,16,3,1,8,3]{1,4,5,2,0,3:T(8,128)(2,1)S(1)} %copy.69, pred[8,3]{0,1:T(4,128)(4,1)S(1)} %copy-done.5), kind=kOutput, calls=%fused_computation.14 | convolution fusion | flops 340916736 | bytes 1352856 | tf_op jit(solution)/shard_map/conv_general_dilated | solution.py:32
  50.3 24.4 %all_to_all.18 = bf16[32,1,512,1,16]{2,4,3,1,0:T(8,128)(2,1)S(1)} all-to-all(bf16[32,1,512,1,16]{2,4,3,1,0:T(8,128)(2,1)S(1)} %copy.71), channel_id=1, replica_groups=mesh['row'=32,'col'=8] {'row'}, dimensions={0} | all-to-all | bytes 1048576 | tf_op jit(solution)/shard_map/all_to_all | solution.py:27
  74.8 1.5 convolution_bitcast_fusion
  79.7 4.2 %collective-permute-start.2 = (bf16[1,32,8,128]{1,2,3,0:T(8,128)(2,1)S(1)}, bf16[1,32,8,128]{1,2,3,0:T(8,128)(2,1)S(1)}, u32[]{:S(2)}, u32[]{:S(2)}) collective-permute-start(bf16[1,32,8,128]{1,2,3,0:T(8,128)(2,1)S(1)} %get-tuple-element.7), channel_id=1, source_target_pairs={{0,8},{8,16},{16,24},{24,32},{32,40},{40,48},{48,56},{56,64},{64,7... | collective-permute-start | bytes 196616 | tf_op jit(solution)/shard_map/ppermute | solution.py:12
  83.9 1.9 %collective-permute-start.3 = (bf16[1,32,8,128]{1,2,3,0:T(8,128)(2,1)S(1)}, bf16[1,32,8,128]{1,2,3,0:T(8,128)(2,1)S(1)}, u32[]{:S(2)}, u32[]{:S(2)}) collective-permute-start(bf16[1,32,8,128]{1,2,3,0:T(8,128)(2,1)S(1)} %get-tuple-element.8), channel_id=1, source_target_pairs={{8,0},{16,8},{24,16},{32,24},{40,32},{48,40},{56,48},{64,56},{72,6... | collective-permute-start | bytes 196616 | tf_op jit(solution)/shard_map/ppermute | solution.py:15
  85.8 3.6 %collective-permute-done.2 = bf16[1,32,8,128]{1,2,3,0:T(8,128)(2,1)S(1)} collective-permute-done((bf16[1,32,8,128]{1,2,3,0:T(8,128)(2,1)S(1)}, bf16[1,32,8,128]{1,2,3,0:T(8,128)(2,1)S(1)}, u32[]{:S(2)}, u32[]{:S(2)}) %collective-permute-start.2) | collective-permute-done | bytes 65568 | tf_op jit(solution)/shard_map/ppermute | solution.py:12
  89.4 12.5 %collective-permute-done.3 = bf16[1,32,8,128]{1,2,3,0:T(8,128)(2,1)S(1)} collective-permute-done((bf16[1,32,8,128]{1,2,3,0:T(8,128)(2,1)S(1)}, bf16[1,32,8,128]{1,2,3,0:T(8,128)(2,1)S(1)}, u32[]{:S(2)}, u32[]{:S(2)}) %collective-permute-start.3) | collective-permute-done | bytes 65568 | tf_op jit(solution)/shard_map/ppermute | solution.py:15
  102.5 1.5 copy-done.2
  106.0 3.3 %collective-permute-start.5 = (bf16[10,32,1,128]{3,1,2,0:T(8,128)(2,1)S(1)}, bf16[10,32,1,128]{3,1,2,0:T(8,128)(2,1)S(1)}, u32[]{:S(2)}, u32[]{:S(2)}) collective-permute-start(bf16[10,32,1,128]{3,1,2,0:T(8,128)(2,1)S(1)} %copy.75), channel_id=1, source_target_pairs={{1,0},{2,1},{3,2},{4,3},{5,4},{6,5},{7,6},{9,8},{10,9},{11,10},{12... | collective-permute-start | bytes 245768 | tf_op jit(solution)/shard_map/ppermute | solution.py:15
  109.3 3.6 %collective-permute-start.4 = (bf16[10,32,1,128]{3,1,2,0:T(8,128)(2,1)S(1)}, bf16[10,32,1,128]{3,1,2,0:T(8,128)(2,1)S(1)}, u32[]{:S(2)}, u32[]{:S(2)}) collective-permute-start(bf16[10,32,1,128]{3,1,2,0:T(8,128)(2,1)S(1)} %copy.74), channel_id=1, source_target_pairs={{0,1},{1,2},{2,3},{3,4},{4,5},{5,6},{6,7},{8,9},{9,10},{10,11},{11... | collective-permute-start | bytes 245768 | tf_op jit(solution)/shard_map/ppermute | solution.py:12
  113.0 3.3 %copy.76 = bf16[10,32,8,128]{3,1,2,0:T(8,128)(2,1)S(1)} copy(bf16[10,32,8,128]{1,2,3,0:T(8,128)(2,1)} %copy-done.2) | data formatting | bytes 1310720 | tf_op jit(solution)/shard_map/concatenate | solution.py:16
  116.4 1.8 %pad.7 = bf16[10,32,10,1,136]{4,1,2,0,3:T(8,128)(2,1)} pad(bf16[10,32,10,1,128]{4,1,2,0,3:T(8,128)(2,1)S(1)} %maximum_bitcast_fusion, bf16[]{:T(256)} %constant.13.clone.1), padding=0_0x0_0x0_0x0_0x1_7 | pad | bytes 1689602 | tf_op jit(solution)/shard_map/broadcast_in_dim | solution.py:33
  118.2 8.7 %reshape.75 = bf16[10,32,10,1,8,17]{5,4,1,2,0,3:T(8,128)(2,1)} reshape(bf16[10,32,10,1,136]{4,1,2,0,3:T(8,128)(2,1)} %pad.7) | data formatting | bytes 1740800 | tf_op jit(solution)/shard_map/conv_general_dilated | solution.py:32
  126.9 10.2 %copy.78 = bf16[10,32,10,1,8,17]{1,4,5,2,0,3:T(8,128)(2,1)} copy(bf16[10,32,10,1,8,17]{5,4,1,2,0,3:T(8,128)(2,1)} %reshape.75) | data formatting | bytes 1740800 | tf_op jit(solution)/shard_map/conv_general_dilated | solution.py:32
  138.2 9.6 %broadcast_select_fusion = f32[8,8,8,17,32]{4,2,3,1,0:T(8,128)S(1)} fusion(pred[8,17]{0,1:T(8,128)(4,1)S(1)} %copy-done.4, bf16[3,3,3,32,32]{4,3,2,1,0:T(8,128)(2,1)S(1)} %copy-done.3, bf16[10,32,10,1,7,2]{1,4,5,2,0,3:T(8,128)(2,1)S(1)} %slice.26, bf16[10,32,10,1,8,17]{1,4,5,2,0,3:T(8,128)(2,1)} %copy.78), kind=kOutput, calls=%fused_computation.10 | convolution fusion | flops 484493312 | bytes 2129544 | tf_op jit(solution)/shard_map/conv_general_dilated | solution.py:32
  148.6 2.2 %slice.27 = f32[8,8,1,128,32]{4,1,3,0,2:T(8,128)} slice(f32[8,8,1,136,32]{4,1,3,0,2:T(8,128)S(1)} %bitcast.77), slice={[0:8], [0:8], [0:1], [0:128], [0:32]} | slice | bytes 2097152 | tf_op jit(solution)/shard_map/conv_general_dilated | solution.py:32
  150.8 2.8 %copy.83 = f32[8,8,1,128,32]{3,1,4,0,2:T(8,128)S(1)} copy(f32[8,8,1,128,32]{4,1,3,0,2:T(8,128)} %slice.27) | data formatting | bytes 2097152
  (47 shorter events, 15.7 us)
Async XLA Ops:
  0.0 74.8 %copy-start = (bf16[4,4,4,32,512]{4,3,2,1,0:T(8,128)(2,1)S(1)}, bf16[4,4,4,32,512]{4,3,2,1,0:T(8,128)(2,1)}, u32[]{:S(2)}) copy-start(bf16[4,4,4,32,512]{4,3,2,1,0:T(8,128)(2,1)} %param.8) | copy-start | bytes 6291460
  15.0 32.6 %copy-start.5 = (pred[8,3]{0,1:T(4,128)(4,1)S(1)}, pred[8,3]{0,1:T(4,128)(4,1)}, u32[]{:S(2)}) copy-start(pred[8,3]{0,1:T(4,128)(4,1)} %constant.27) | copy-start | bytes 76
  37.8 7.3 %collective-permute-start.1 = (bf16[32,16,1,16]{1,0,3,2:T(8,128)(2,1)S(1)}, bf16[32,16,1,16]{1,0,3,2:T(8,128)(2,1)S(1)}, u32[]{:S(2)}, u32[]{:S(2)}) collective-permute-start(bf16[32,16,1,16]{1,0,3,2:T(8,128)(2,1)S(1)} %all_to_all.13), channel_id=1, source_target_pairs={{1,0},{2,1},{3,2},{4,3},{5,4},{6,5},{7,6},{9,8},{10,9},{11,10},{12... | collective-permute-start | bytes 49160 | tf_op jit(solution)/shard_map/ppermute | solution.py:15
  41.8 4.5 %collective-permute-start = (bf16[32,16,1,16]{1,0,3,2:T(8,128)(2,1)S(1)}, bf16[32,16,1,16]{1,0,3,2:T(8,128)(2,1)S(1)}, u32[]{:S(2)}, u32[]{:S(2)}) collective-permute-start(bf16[32,16,1,16]{1,0,3,2:T(8,128)(2,1)S(1)} %all_to_all.13), channel_id=1, source_target_pairs={{0,1},{1,2},{2,3},{3,4},{4,5},{5,6},{6,7},{8,9},{9,10},{10,11},{11... | collective-permute-start | bytes 49160 | tf_op jit(solution)/shard_map/ppermute | solution.py:12
  77.7 1.6 %copy-start.1 = (bf16[8,32,8,128]{1,2,3,0:T(8,128)(2,1)S(1)}, bf16[8,32,8,128]{1,2,3,0:T(8,128)(2,1)}, u32[]{:S(2)}) copy-start(bf16[8,32,8,128]{1,2,3,0:T(8,128)(2,1)} %copy.62) | copy-start | bytes 1572868
  79.7 9.7 %collective-permute-start.2 = (bf16[1,32,8,128]{1,2,3,0:T(8,128)(2,1)S(1)}, bf16[1,32,8,128]{1,2,3,0:T(8,128)(2,1)S(1)}, u32[]{:S(2)}, u32[]{:S(2)}) collective-permute-start(bf16[1,32,8,128]{1,2,3,0:T(8,128)(2,1)S(1)} %get-tuple-element.7), channel_id=1, source_target_pairs={{0,8},{8,16},{16,24},{24,32},{32,40},{40,48},{48,56},{56,64},{64,7... | collective-permute-start | bytes 196616 | tf_op jit(solution)/shard_map/ppermute | solution.py:12
  83.9 18.0 %collective-permute-start.3 = (bf16[1,32,8,128]{1,2,3,0:T(8,128)(2,1)S(1)}, bf16[1,32,8,128]{1,2,3,0:T(8,128)(2,1)S(1)}, u32[]{:S(2)}, u32[]{:S(2)}) collective-permute-start(bf16[1,32,8,128]{1,2,3,0:T(8,128)(2,1)S(1)} %get-tuple-element.8), channel_id=1, source_target_pairs={{8,0},{16,8},{24,16},{32,24},{40,32},{48,40},{56,48},{64,56},{72,6... | collective-permute-start | bytes 196616 | tf_op jit(solution)/shard_map/ppermute | solution.py:15
  102.5 1.5 copy-start.2
  106.0 10.3 %collective-permute-start.5 = (bf16[10,32,1,128]{3,1,2,0:T(8,128)(2,1)S(1)}, bf16[10,32,1,128]{3,1,2,0:T(8,128)(2,1)S(1)}, u32[]{:S(2)}, u32[]{:S(2)}) collective-permute-start(bf16[10,32,1,128]{3,1,2,0:T(8,128)(2,1)S(1)} %copy.75), channel_id=1, source_target_pairs={{1,0},{2,1},{3,2},{4,3},{5,4},{6,5},{7,6},{9,8},{10,9},{11,10},{12... | collective-permute-start | bytes 245768 | tf_op jit(solution)/shard_map/ppermute | solution.py:15
  109.3 7.0 %collective-permute-start.4 = (bf16[10,32,1,128]{3,1,2,0:T(8,128)(2,1)S(1)}, bf16[10,32,1,128]{3,1,2,0:T(8,128)(2,1)S(1)}, u32[]{:S(2)}, u32[]{:S(2)}) collective-permute-start(bf16[10,32,1,128]{3,1,2,0:T(8,128)(2,1)S(1)} %copy.74), channel_id=1, source_target_pairs={{0,1},{1,2},{2,3},{3,4},{4,5},{5,6},{6,7},{8,9},{9,10},{10,11},{11... | collective-permute-start | bytes 245768 | tf_op jit(solution)/shard_map/ppermute | solution.py:12
  126.9 11.3 %copy-start.3 = (bf16[3,3,3,32,32]{4,3,2,1,0:T(8,128)(2,1)S(1)}, bf16[3,3,3,32,32]{4,3,2,1,0:T(8,128)(2,1)}, u32[]{:S(2)}) copy-start(bf16[3,3,3,32,32]{4,3,2,1,0:T(8,128)(2,1)} %param.9) | copy-start | bytes 165892
  126.9 11.3 %copy-start.4 = (pred[8,17]{0,1:T(8,128)(4,1)S(1)}, pred[8,17]{0,1:T(8,128)(4,1)}, u32[]{:S(2)}) copy-start(pred[8,17]{0,1:T(8,128)(4,1)} %constant.26) | copy-start | bytes 412
where the time goes:
time: 156 us; the launch traced here: 155 us
  local copies, waits for them, and re-layouts  48 us (31%)
  blocking collectives  44.6 us (29%)
  starting transfers between devices  19.6 us (13%)
  waiting for transfers between devices  18 us (12%)
  matrix products  15.5 us (10%)
  other arithmetic  8.78 us (6%)
    all_to_all x1, blocking collectives, sent_and_summed(): lax.all_to_all(tiles, axis, split_axis=0, concat_axis=0, tiled=True)  24.4 us
    conv_general_dilated x7, local copies, waits for them, and re-layouts, convolve(): lax.conv_general_dilated(padded[None], kernel, (1, 1, 1), ((0, 0), (0, 0)...  23.7 us
    all_to_all x1, blocking collectives, body(): lax.all_to_all(lowered, 'row', split_axis=1, concat_axis=0, tiled=True)  20.2 us
    ppermute x3, waiting for transfers between devices, with_halo(): lax.ppermute(lax.slice_in_dim(block, 0, width, axis=dim), axis, backward)  13.2 us
    conv_general_dilated x2, matrix products, convolve(): lax.conv_general_dilated(padded[None], kernel, (1, 1, 1), ((0, 0), (0, 0)...  11.7 us
    unnamed x18, local copies, waits for them, and re-layouts  10.4 us
    ppermute x3, starting transfers between devices, with_halo(): lax.ppermute(lax.slice_in_dim(block, block.shape[dim] - width, None, axis...  10.3 us
    ppermute x3, starting transfers between devices, with_halo(): lax.ppermute(lax.slice_in_dim(block, 0, width, axis=dim), axis, backward)  9.27 us
  transfers between devices with their start and end apart: 6, of which 4 were waited for; matrix products, arithmetic and copies ran while one was open for 2% of the time, Pallas kernels for 0%

commit v1 on v0

v1 whole, which is shorter than its diff:
```python
import jax
import jax.numpy as jnp
from jax import lax
from jax.experimental import pallas as pl
from jax.experimental.pallas import tpu as pltpu
from jax.sharding import PartitionSpec as P

MESH = pl.DeviceIdType.MESH
F32 = jnp.float32
BF16 = jnp.bfloat16
ROWS, COLS, GROUP = 32, 8, 4
C1, CB, WIDTH = 32, 512, 128
DEP, HGT, WB = 8, 8, 16
CIN = CB // ROWS
NT = (((1,), (1,)), ((), ()))


def iota(shape, dim):
    return lax.broadcasted_iota(jnp.int32, shape, dim)


def ones_where(mask):
    return jnp.where(mask, 1.0, 0.0).astype(BF16)


def silu(v):
    return v / (1.0 + jnp.exp(-v))


def dot(a, b):
    return jnp.dot(a, b, preferred_element_type=F32)


def dot_nt(a, b):
    return lax.dot_general(a, b, NT, preferred_element_type=F32)


def kernel(
    feat_hbm, down_hbm, bott_hbm, up_hbm, dec_hbm, out_ref,
    feat, down, up, dec, wg, lowered, tiles, part, arrived, band, band_h,
    slabs, edges_out, edges_in, edges, accs,
    load_sem, w_send, w_recv, a_send, a_recv, h_send, h_recv, p_send, p_recv, j_send, j_recv,
):
    row, col = lax.axis_index("row"), lax.axis_index("col")
    lane = row % GROUP
    half = (row // GROUP) % 2

    def at_row(step):
        return (row + step + ROWS) % ROWS

    def at_col(step):
        return (col + step + COLS) % COLS

    def device(r, c):
        return {"row": r, "col": c}

    loads = [
        pltpu.make_async_copy(src, dst, load_sem.at[i])
        for i, (src, dst) in enumerate(
            [(feat_hbm, feat), (down_hbm, down), (dec_hbm, dec), (up_hbm, up)]
        )
    ]
    for load in loads:
        load.start()

    def weight_slot(owner_lane):
        start = pl.multiple_of(half * (GROUP * CIN) + owner_lane * CIN, CIN)
        return wg.at[:, pl.ds(start, CIN), :]

    def weight_piece(lane_to):
        return bott_hbm.at[:, :, pl.ds(pl.multiple_of(lane_to * 128, 128), 128)]

    own_weight = pltpu.make_async_copy(weight_piece(lane), weight_slot(lane), load_sem.at[4])
    own_weight.start()

    barrier = pltpu.get_barrier_semaphore()

    def greet(r, c):
        pl.semaphore_signal(barrier, inc=1, device_id=device(r, c), device_id_type=MESH)

    @pl.loop(1, ROWS)
    def _(j):
        greet(at_row(j), col)

    for dr in (-1, 0, 1):
        for dc in (-1, 1):
            greet(at_row(dr), at_col(dc))

    rest = pl.multiple_of((1 - half) * (GROUP * CIN), GROUP * CIN)
    wg[:, pl.ds(rest, GROUP * CIN), :] = jnp.zeros((27, GROUP * CIN, 128), BF16)
    tiles[:, 0] = jnp.zeros((3, WB, 128), BF16)
    tiles[:, ROWS + 1] = jnp.zeros((3, WB, 128), BF16)

    loads[0].wait()
    r_, c_ = iota((128, 256), 0), iota((128, 256), 1)
    pool_h = ones_where(((r_ % C1) == (c_ // HGT)) & ((r_ // C1) == (c_ % HGT) // 2))
    pool_h = jnp.concatenate([pool_h, pool_h], axis=1)
    r_, c_ = iota((64, WIDTH), 0), iota((64, WIDTH), 1)
    pool_w = jnp.where((c_ // 2) == (r_ % WB) * 4 + r_ // WB, 0.125, 0.0).astype(BF16)
    pooled = []
    for a in range(4):
        pair = feat[2 * a : 2 * a + 2].reshape(512, WIDTH)
        pooled.append(dot_nt(pool_w, dot(pool_h, pair).astype(BF16)).astype(BF16))
    pooled = jnp.concatenate(pooled, axis=1)

    pl.semaphore_wait(barrier, ROWS - 1 + 6)

    weight_sends = []
    for j in range(1, GROUP):
        to = (lane + j) % GROUP
        copy = pltpu.make_async_remote_copy(
            src_ref=weight_piece(to),
            dst_ref=weight_slot(lane),
            send_sem=w_send.at[j - 1],
            recv_sem=w_recv.at[j - 1],
            device_id=device(row - lane + to, col),
            device_id_type=MESH,
        )
        copy.start()
        weight_sends.append(copy)

    loads[1].wait()
    total = jnp.zeros((WB, CB), F32)
    for c in range(4):
        total += dot(pooled[c * WB : (c + 1) * WB], down[:, c].reshape(512, CB))
    low = silu(total).astype(BF16)
    for k in range(4):
        lowered[k] = low[:, k * 128 : (k + 1) * 128]

    def tile_copy(j):
        to = at_row(j)
        return pltpu.make_async_remote_copy(
            src_ref=lowered.at[to // 8],
            dst_ref=tiles.at[1, 1 + row],
            send_sem=a_send,
            recv_sem=a_recv,
            device_id=device(to, col),
            device_id_type=MESH,
        )

    @pl.loop(1, ROWS)
    def _(j):
        tile_copy(j).start()

    tiles[1, 1 + row] = lowered[row // 8]

    loads[2].wait()
    r_, c_ = iota((256, C1), 0), iota((256, C1), 1)
    spread_o = ones_where((r_ // HGT) == c_)
    r_, c_ = iota((C1, 256), 0), iota((C1, 256), 1)
    spread_c = ones_where((c_ // HGT) == r_)
    shift = (iota((256, 256), 1) % HGT) - (iota((256, 256), 0) % HGT)
    h_of = iota((256, C1), 0) % HGT
    for kd in range(3):
        for kw in range(3):
            total = jnp.zeros((256, 256), F32)
            sides = []
            for kh in range(3):
                taps = dot_nt(spread_o, dec[(kd * 3 + kh) * 3 + kw]).astype(BF16)
                total = jnp.where(shift == kh - 1, dot(taps, spread_c), total)
                if kh != 1:
                    edge = 0 if kh == 0 else HGT - 1
                    sides.append(jnp.where(h_of == edge, taps.astype(F32), 0.0))
            at = kd * 3 + kw
            band[:, at * 256 : (at + 1) * 256] = total.astype(BF16)
            band_h[:, at * 64 : (at + 1) * 64] = jnp.concatenate(sides, axis=1).astype(BF16)

    def all_tiles(ref, send, recv):
        span = ref.at[pl.ds(1, ROWS - 1)]
        return pltpu.make_async_remote_copy(
            src_ref=span, dst_ref=span, send_sem=send, recv_sem=recv,
            device_id=device(at_row(1), col), device_id_type=MESH,
        )

    all_tiles(tiles.at[1], a_send, a_recv).wait_recv()

    halo_sends = []
    for i, step in enumerate((-1, 1)):
        copy = pltpu.make_async_remote_copy(
            src_ref=tiles.at[1, pl.ds(1, ROWS)],
            dst_ref=tiles.at[1 - step, pl.ds(1, ROWS)],
            send_sem=h_send.at[i],
            recv_sem=h_recv.at[i],
            device_id=device(row, at_col(step)),
            device_id_type=MESH,
        )
        copy.start()
        halo_sends.append(copy)

    own_weight.wait()
    for copy in weight_sends:
        copy.wait()

    def patches(heights):
        return jnp.concatenate(
            [tiles[b, a : a + ROWS].reshape(ROWS * WB, 128) for a in range(3) for b in heights], axis=1
        )

    def taps_of(heights):
        return jnp.concatenate(
            [
                jnp.concatenate([wg[a * 9 + b * 3 + c] for a in range(3) for b in heights], axis=0)
                for c in range(3)
            ],
            axis=1,
        )

    partial = dot(patches((1,)), taps_of((1,)))
    for copy in halo_sends:
        copy.wait()

    @pl.when(col == 0)
    def _():
        tiles[0] = jnp.zeros((ROWS + 2, WB, 128), BF16)

    @pl.when(col == COLS - 1)
    def _():
        tiles[2] = jnp.zeros((ROWS + 2, WB, 128), BF16)

    partial += dot(patches((0, 2)), taps_of((0, 2)))
    w_of = iota((ROWS * WB, 128), 0) % WB
    before = pltpu.roll(partial[:, :128], 1, 0)
    after = pltpu.roll(partial[:, 256:], ROWS * WB - 1, 0)
    summed = partial[:, 128:256] + jnp.where(w_of == 0, 0.0, before) + jnp.where(w_of == WB - 1, 0.0, after)
    part[...] = summed.astype(BF16).reshape(ROWS, WB, 128)

    def part_copy(j):
        to = at_row(j)
        return pltpu.make_async_remote_copy(
            src_ref=part.at[to],
            dst_ref=arrived.at[row],
            send_sem=p_send,
            recv_sem=p_recv,
            device_id=device(to, col),
            device_id_type=MESH,
        )

    @pl.loop(1, ROWS)
    def _(j):
        part_copy(j).start()

    arrived[row] = part[row]
    r_, c_ = iota((512, WB), 0), iota((512, WB), 1)
    spread_w = ones_where((((r_ % WIDTH) // 8) == c_) & ((((r_ % WIDTH) // 2) % 4) == (r_ // WIDTH)))
    r_, c_ = iota((256, 128), 0), iota((256, 128), 1)
    raise_h = ones_where(((c_ % C1) == (r_ // HGT)) & ((c_ // C1) == (r_ % HGT) // 2))
    loads[3].wait()
    all_tiles(arrived, p_send, p_recv).wait_recv()

    groups = arrived[...].reshape(ROWS // GROUP, GROUP, WB, 128).astype(F32).sum(axis=0)
    middle = silu(jnp.concatenate([groups[k] for k in range(GROUP)], axis=1)).astype(BF16)
    spread = dot(spread_w, middle).astype(BF16)
    raised = jnp.zeros((512, WIDTH), F32)
    for c in range(4):
        raised += dot_nt(up[:, c].reshape(512, CB), spread[c * WIDTH : (c + 1) * WIDTH])
    raised = raised.astype(BF16)

    v_of = iota((256, WIDTH), 1)

    def store_slab(i, value, rows=256):
        v_ = v_of[:rows]
        return (
            jnp.where(v_ == 0, 0.0, pltpu.roll(value, 1, 1)).astype(BF16),
            jnp.where(v_ == WIDTH - 1, 0.0, pltpu.roll(value, WIDTH - 1, 1)).astype(BF16),
        )

    r_, c_ = iota((64, 256), 0), iota((64, 256), 1)
    pick = ones_where(((c_ // HGT) == (r_ % C1)) & ((c_ % HGT) == (r_ // C1) * (HGT - 1)))
    for d in range(DEP):
        if d % 2 == 0:
            lift = dot(raise_h, raised[(d // 2) * 128 : (d // 2 + 1) * 128])
        joined = (feat[d].astype(F32) + lift).astype(BF16)
        slabs[1 + d, 1] = joined
        rim = dot(pick, joined).astype(BF16)
        edges_out[0, d] = rim[:C1]
        edges_out[1, d] = rim[C1:]

    moves = []
    for side, step in ((0, -1), (1, 1)):
        moves.append((edges_out.at[side], edges_in.at[1 - side, pl.ds(1, DEP)], row, at_col(step)))
        for d, hop, slot in ((0, -1, DEP + 1), (DEP - 1, 1, 0)):
            moves.append((edges_out.at[side, d], edges_in.at[1 - side, slot], at_row(hop), at_col(step)))
    for d, hop, slot in ((1, -1, DEP + 1), (DEP, 1, 0)):
        moves.append((slabs.at[d, 1], slabs.at[slot, 1], at_row(hop), col))
    joined_sends = []
    for i, (src, dst, r, c) in enumerate(moves):
        copy = pltpu.make_async_remote_copy(
            src_ref=src, dst_ref=dst, send_sem=j_send.at[i], recv_sem=j_recv.at[i],
            device_id=device(r, c), device_id_type=MESH,
        )
        copy.start()
        joined_sends.append(copy)

    for d in range(1, DEP + 1):
        left, right = store_slab(d, slabs[d, 1].astype(F32))
        slabs[d, 0] = left
        slabs[d, 2] = right
    for d in range(1, DEP - 1):
        accs[d] = dot(band[...], slabs[d : d + 3].reshape(9 * 256, WIDTH))

    for copy in joined_sends:
        copy.wait()

    @pl.when(row == 0)
    def _():
        slabs[0, 1] = jnp.zeros((256, WIDTH), BF16)
        edges_in[:, 0] = jnp.zeros((2, C1, WIDTH), BF16)

    @pl.when(row == ROWS - 1)
    def _():
        slabs[DEP + 1, 1] = jnp.zeros((256, WIDTH), BF16)
        edges_in[:, DEP + 1] = jnp.zeros((2, C1, WIDTH), BF16)

    @pl.when(col == 0)
    def _():
        edges_in[0] = jnp.zeros((DEP + 2, C1, WIDTH), BF16)

    @pl.when(col == COLS - 1)
    def _():
        edges_in[1] = jnp.zeros((DEP + 2, C1, WIDTH), BF16)

    for d in (0, DEP + 1):
        left, right = store_slab(d, slabs[d, 1].astype(F32))
        slabs[d, 0] = left
        slabs[d, 2] = right
    for d in range(DEP + 2):
        rim = jnp.concatenate([edges_in[0, d], edges_in[1, d]], axis=0)
        left, right = store_slab(d, rim.astype(F32), 64)
        edges[d, 0] = left
        edges[d, 1] = rim
        edges[d, 2] = right
    for d in range(DEP):
        if d in (0, DEP - 1):
            total = dot(band[...], slabs[d : d + 3].reshape(9 * 256, WIDTH))
        else:
            total = accs[d]
        total += dot(band_h[...], edges[d : d + 3].reshape(9 * 64, WIDTH))
        out_ref[d] = silu(total).astype(BF16)

    all_tiles(tiles.at[1], a_send, a_recv).wait_send()
    all_tiles(arrived, p_send, p_recv).wait_send()


def body(features, down_weight, bott_weight, up_weight, dec_weight):
    dma = pltpu.SemaphoreType.DMA
    out = pl.pallas_call(
        kernel,
        out_shape=jax.ShapeDtypeStruct((DEP, 256, WIDTH), BF16),
        in_specs=[pl.BlockSpec(memory_space=pl.ANY)] * 5,
        out_specs=pl.BlockSpec(memory_space=pltpu.VMEM),
        scratch_shapes=[
            pltpu.VMEM((DEP, 256, WIDTH), BF16),
            pltpu.VMEM((16, 4, C1, CB), BF16),
            pltpu.VMEM((16, 4, C1, CB), BF16),
            pltpu.VMEM((27, C1, C1), BF16),
            pltpu.VMEM((27, 128, 128), BF16),
            pltpu.VMEM((4, WB, 128), BF16),
            pltpu.VMEM((3, ROWS + 2, WB, 128), BF16),
            pltpu.VMEM((ROWS, WB, 128), BF16),
            pltpu.VMEM((ROWS, WB, 128), BF16),
            pltpu.VMEM((256, 9 * 256), BF16),
            pltpu.VMEM((256, 9 * 64), BF16),
            pltpu.VMEM((DEP + 2, 3, 256, WIDTH), BF16),
            pltpu.VMEM((2, DEP, C1, WIDTH), BF16),
            pltpu.VMEM((2, DEP + 2, C1, WIDTH), BF16),
            pltpu.VMEM((DEP + 2, 3, 64, WIDTH), BF16),
            pltpu.VMEM((DEP, 256, WIDTH), F32),
            dma((5,)), dma((3,)), dma((3,)), dma, dma, dma((2,)), dma((2,)), dma, dma, dma((8,)), dma((8,)),
        ],
        compiler_params=pltpu.CompilerParams(
            collective_id=0, has_side_effects=True, vmem_limit_bytes=48 * 1024 * 1024
        ),
        name="encode_decode",
    )(
        features.reshape(DEP, 256, WIDTH),
        down_weight.reshape(16, 4, C1, CB),
        bott_weight.reshape(27, CIN, CB),
        up_weight.reshape(16, 4, C1, CB),
        dec_weight.reshape(27, C1, C1),
    )
    return out.reshape(features.shape)


def solution(mesh):
    placed = (P("row", None, "col", None), P(), P(None, None, None, "row", None), P(), P())
    return jax.shard_map(
        body, mesh=mesh, in_specs=placed, out_specs=P("row", None, "col", None), check_vma=False
    )
```

time: 156 us -> 58.2 us (0.37)
  the two profiles are of different devices: /device:TPU:63 before, /device:TPU:1 now
where the time goes in v1:
time: 58.2 us; the launch traced here: 58 us
  Pallas kernels  51 us (88%)
  local copies, waits for them, and re-layouts  6.97 us (12%)
    pallas_call x1, Pallas kernels, body(): pl.pallas_call(kernel, out_shape=jax.ShapeDtypeStruct((DEP, 256, WIDTH),...  51 us
    unnamed x11, local copies, waits for them, and re-layouts  6.97 us

profile of v1, /device:TPU:1, one launch (start us, length us, event | category | flops | bytes accessed | tf_op | source)
XLA Modules:
  0.0 58.0 jit_solution(16864270842110202553)
XLA Ops:
  0.0 0.0 copy-start
  0.0 1.6 %copy-done = bf16[4,4,4,32,512]{4,3,2,1,0:T(8,128)(2,1)S(1)} copy-done((bf16[4,4,4,32,512]{4,3,2,1,0:T(8,128)(2,1)S(1)}, bf16[4,4,4,32,512]{4,3,2,1,0:T(8,128)(2,1)}, u32[]{:S(2)}) %copy-start) | copy-done | bytes 2097176
  1.6 0.0 copy-start.1
  1.6 1.6 %copy-done.1 = bf16[4,4,4,32,512]{4,3,2,1,0:T(8,128)(2,1)S(1)} copy-done((bf16[4,4,4,32,512]{4,3,2,1,0:T(8,128)(2,1)S(1)}, bf16[4,4,4,32,512]{4,3,2,1,0:T(8,128)(2,1)}, u32[]{:S(2)}) %copy-start.1) | copy-done | bytes 2097176
  3.2 0.0 copy-start.2
  3.2 1.0 %copy-done.2 = bf16[8,32,8,128]{3,2,1,0:T(8,128)(2,1)S(1)} copy-done((bf16[8,32,8,128]{3,2,1,0:T(8,128)(2,1)S(1)}, bf16[8,32,8,128]{3,2,1,0:T(8,128)(2,1)}, u32[]{:S(2)}) %copy-start.2) | copy-done | bytes 524312
  4.2 0.0 copy-start.3
  4.2 1.0 %copy-done.3 = bf16[3,3,3,16,512]{4,3,2,1,0:T(8,128)(2,1)S(1)} copy-done((bf16[3,3,3,16,512]{4,3,2,1,0:T(8,128)(2,1)S(1)}, bf16[3,3,3,16,512]{4,3,2,1,0:T(8,128)(2,1)}, u32[]{:S(2)}) %copy-start.3) | copy-done | bytes 442392
  5.2 0.0 copy-start.4
  5.2 0.9 %copy-done.4 = bf16[3,3,3,32,32]{4,3,2,1,0:T(8,128)(2,1)S(1)} copy-done((bf16[3,3,3,32,32]{4,3,2,1,0:T(8,128)(2,1)S(1)}, bf16[3,3,3,32,32]{4,3,2,1,0:T(8,128)(2,1)}, u32[]{:S(2)}) %copy-start.4) | copy-done | bytes 55320
  6.2 51.0 %encode_decode.1 = bf16[8,256,128]{2,1,0:T(8,128)(2,1)S(1)} custom-call(bf16[8,256,128]{2,1,0:T(8,128)(2,1)S(1)} %bitcast.9, bf16[16,4,32,512]{3,2,1,0:T(8,128)(2,1)S(1)} %bitcast.7, bf16[27,16,512]{2,1,0:T(8,128)(2,1)S(1)} %bitcast.10, bf16[16,4,32,512]{3,2,1,0:T(8,128)(2,1)S(1)} %bitcast.8, bf16[27,32,32]{2,1,0:T(8,128)(2,1)S(1)} %bitcast.11), custom_call_target="tpu_custom_call" | custom-call | tf_op jit(solution)/shard_map/encode_decode/pallas_call | solution.py:346
  57.2 0.8 %copy.7 = bf16[8,32,8,128]{3,2,1,0:T(8,128)(2,1)} copy(bf16[8,32,8,128]{3,2,1,0:T(8,128)(2,1)S(1)} %bitcast.6) | data formatting | bytes 1048576
Async XLA Ops:
  0.0 1.6 %copy-start = (bf16[4,4,4,32,512]{4,3,2,1,0:T(8,128)(2,1)S(1)}, bf16[4,4,4,32,512]{4,3,2,1,0:T(8,128)(2,1)}, u32[]{:S(2)}) copy-start(bf16[4,4,4,32,512]{4,3,2,1,0:T(8,128)(2,1)} %param.6) | copy-start | bytes 6291460
  1.6 1.6 %copy-start.1 = (bf16[4,4,4,32,512]{4,3,2,1,0:T(8,128)(2,1)S(1)}, bf16[4,4,4,32,512]{4,3,2,1,0:T(8,128)(2,1)}, u32[]{:S(2)}) copy-start(bf16[4,4,4,32,512]{4,3,2,1,0:T(8,128)(2,1)} %param.8) | copy-start | bytes 6291460
  3.2 1.0 %copy-start.2 = (bf16[8,32,8,128]{3,2,1,0:T(8,128)(2,1)S(1)}, bf16[8,32,8,128]{3,2,1,0:T(8,128)(2,1)}, u32[]{:S(2)}) copy-start(bf16[8,32,8,128]{3,2,1,0:T(8,128)(2,1)} %param.5) | copy-start | bytes 1572868
  4.2 1.0 %copy-start.3 = (bf16[3,3,3,16,512]{4,3,2,1,0:T(8,128)(2,1)S(1)}, bf16[3,3,3,16,512]{4,3,2,1,0:T(8,128)(2,1)}, u32[]{:S(2)}) copy-start(bf16[3,3,3,16,512]{4,3,2,1,0:T(8,128)(2,1)} %param.7) | copy-start | bytes 1327108
  5.2 0.9 %copy-start.4 = (bf16[3,3,3,32,32]{4,3,2,1,0:T(8,128)(2,1)S(1)}, bf16[3,3,3,32,32]{4,3,2,1,0:T(8,128)(2,1)}, u32[]{:S(2)}) copy-start(bf16[3,3,3,32,32]{4,3,2,1,0:T(8,128)(2,1)} %param.9) | copy-start | bytes 165892

commit v2 on v1

v2 whole, which is shorter than its diff:
```python
import jax
import jax.numpy as jnp
from jax import lax
from jax.experimental import pallas as pl
from jax.experimental.pallas import tpu as pltpu
from jax.sharding import PartitionSpec as P

MESH = pl.DeviceIdType.MESH
F32 = jnp.float32
BF16 = jnp.bfloat16
ROWS, COLS, GROUP = 32, 8, 4
C1, CB, WIDTH = 32, 512, 128
DEP, HGT, WB = 8, 8, 16
CIN = CB // ROWS
NT = (((1,), (1,)), ((), ()))


def iota(shape, dim):
    return lax.broadcasted_iota(jnp.int32, shape, dim)


def ones_where(mask):
    return jnp.where(mask, 1.0, 0.0).astype(BF16)


def silu(v):
    return v / (1.0 + jnp.exp(-v))


def dot(a, b):
    return jnp.dot(a, b, preferred_element_type=F32)


def dot_nt(a, b):
    return lax.dot_general(a, b, NT, preferred_element_type=F32)


def hops(offset):
    dz, dx, dy = offset
    return 4 * dz + min(dx, 4 - dx) + min(dy, 4 - dy)


PEERS = sorted(
    [(dz, dx, dy) for dz in range(2) for dx in range(4) for dy in range(4) if dz + dx + dy],
    key=hops,
    reverse=True,
)


def kernel(
    feat_hbm, down_hbm, bott_hbm, up_hbm, dec_hbm, out_ref,
    feat, down, up, dec, wg, lowered, tiles, part, arrived, band, band_h,
    slabs, edges_out, edges_in, edges, accs, feat_in, raised_out, raised_in,
    load_sem, w_send, w_recv, a_send, a_recv, h_send, h_recv, p_send, p_recv, j_send, j_recv, f_send, f_recv,
):
    row, col = lax.axis_index("row"), lax.axis_index("col")
    row_z, row_x, lane = row // 16, (row // GROUP) % 4, row % GROUP
    half = row_x % 2

    def device(r, c):
        return {"row": r, "col": c}

    def peer(offset):
        dz, dx, dy = offset
        return (row_z + dz) % 2 * 16 + (row_x + dx) % 4 * GROUP + (lane + dy) % GROUP

    loads = [
        pltpu.make_async_copy(src, dst, load_sem.at[i])
        for i, (src, dst) in enumerate(
            [(feat_hbm, feat), (down_hbm, down), (dec_hbm, dec), (up_hbm, up)]
        )
    ]
    for load in loads:
        load.start()

    def weight_slot(owner_lane):
        start = pl.multiple_of(half * (GROUP * CIN) + owner_lane * CIN, CIN)
        return wg.at[:, pl.ds(start, CIN), :]

    def weight_piece(lane_to):
        return bott_hbm.at[:, :, pl.ds(pl.multiple_of(lane_to * 128, 128), 128)]

    own_weight = pltpu.make_async_copy(weight_piece(lane), weight_slot(lane), load_sem.at[4])
    own_weight.start()

    barrier = pltpu.get_barrier_semaphore()

    def greet(r, c):
        pl.semaphore_signal(barrier, inc=1, device_id=device(r, c), device_id_type=MESH)

    for offset in PEERS:
        greet(peer(offset), col)
    for dr in (-1, 0, 1):
        for dc in (-1, 1):
            greet((row + dr + ROWS) % ROWS, (col + dc + COLS) % COLS)

    rest = pl.multiple_of((1 - half) * (GROUP * CIN), GROUP * CIN)
    wg[:, pl.ds(rest, GROUP * CIN), :] = jnp.zeros((27, GROUP * CIN, 128), BF16)
    tiles[:, 0] = jnp.zeros((3, WB, 128), BF16)
    tiles[:, ROWS + 1] = jnp.zeros((3, WB, 128), BF16)

    for side, edge in ((0, row == 0), (1, row == ROWS - 1)):
        @pl.when(edge)
        def _():
            feat_in[side] = jnp.zeros((256, WIDTH), BF16)
            raised_in[side] = jnp.zeros((64, WIDTH), BF16)
            edges_in[:, side * (DEP + 1)] = jnp.zeros((2, C1, WIDTH), BF16)

    for side, edge in ((0, col == 0), (1, col == COLS - 1)):
        @pl.when(edge)
        def _():
            tiles[2 * side] = jnp.zeros((ROWS + 2, WB, 128), BF16)
            edges_in[side] = jnp.zeros((DEP + 2, C1, WIDTH), BF16)

    def inside(dr, dc):
        yes = None
        for at, step, count in ((row, dr, ROWS), (col, dc, COLS)):
            if step:
                here = at > 0 if step < 0 else at < count - 1
                yes = here if yes is None else jnp.logical_and(yes, here)
        return yes

    class Shift:
        def __init__(self, src, dst, send, recv, dr, dc):
            self.there, self.back = (dr, dc), (-dr, -dc)
            self.copy = pltpu.make_async_remote_copy(
                src_ref=src, dst_ref=dst, send_sem=send, recv_sem=recv,
                device_id=device((row + dr + ROWS) % ROWS, (col + dc + COLS) % COLS), device_id_type=MESH,
            )

        def start(self):
            @pl.when(inside(*self.there))
            def _():
                self.copy.start()

        def wait(self):
            @pl.when(inside(*self.there))
            def _():
                self.copy.wait_send()

            @pl.when(inside(*self.back))
            def _():
                self.copy.wait_recv()

    loads[0].wait()
    r_, c_ = iota((128, 256), 0), iota((128, 256), 1)
    pool_h = ones_where(((r_ % C1) == (c_ // HGT)) & ((r_ // C1) == (c_ % HGT) // 2))
    pool_h = jnp.concatenate([pool_h, pool_h], axis=1)
    r_, c_ = iota((64, WIDTH), 0), iota((64, WIDTH), 1)
    pool_w = jnp.where((c_ // 2) == (r_ % WB) * 4 + r_ // WB, 0.125, 0.0).astype(BF16)
    pooled = []
    for a in range(4):
        pair = feat[2 * a : 2 * a + 2].reshape(512, WIDTH)
        pooled.append(dot_nt(pool_w, dot(pool_h, pair).astype(BF16)).astype(BF16))
    pooled = jnp.concatenate(pooled, axis=1)

    loads[1].wait()
    total = jnp.zeros((WB, CB), F32)
    for c in range(4):
        total += dot(pooled[c * WB : (c + 1) * WB], down[:, c].reshape(512, CB))
    low = silu(total).astype(BF16)
    for k in range(4):
        lowered[k] = low[:, k * 128 : (k + 1) * 128]

    pl.semaphore_wait(barrier, ROWS - 1 + 6)

    for offset in PEERS:
        to = peer(offset)
        pltpu.make_async_remote_copy(
            src_ref=lowered.at[to // 8],
            dst_ref=tiles.at[1, 1 + row],
            send_sem=a_send,
            recv_sem=a_recv,
            device_id=device(to, col),
            device_id_type=MESH,
        ).start()

    weight_sends = []
    for j in range(1, GROUP):
        to = (lane + j) % GROUP
        copy = pltpu.make_async_remote_copy(
            src_ref=weight_piece(to),
            dst_ref=weight_slot(lane),
            send_sem=w_send.at[j - 1],
            recv_sem=w_recv.at[j - 1],
            device_id=device(row - lane + to, col),
            device_id_type=MESH,
        )
        copy.start()
        weight_sends.append(copy)

    feat_sends = [
        Shift(feat.at[0], feat_in.at[1], f_send.at[0], f_recv.at[0], -1, 0),
        Shift(feat.at[DEP - 1], feat_in.at[0], f_send.at[1], f_recv.at[1], 1, 0),
    ]
    for copy in feat_sends:
        copy.start()

    tiles[1, 1 + row] = lowered[row // 8]

    loads[2].wait()
    r_, c_ = iota((256, C1), 0), iota((256, C1), 1)
    spread_o = ones_where((r_ // HGT) == c_)
    r_, c_ = iota((C1, 256), 0), iota((C1, 256), 1)
    spread_c = ones_where((c_ // HGT) == r_)
    shift = (iota((256, 256), 1) % HGT) - (iota((256, 256), 0) % HGT)
    h_of = iota((256, C1), 0) % HGT
    for kd in range(3):
        for kw in range(3):
            total = jnp.zeros((256, 256), F32)
            sides = []
            for kh in range(3):
                taps = dot_nt(spread_o, dec[(kd * 3 + kh) * 3 + kw]).astype(BF16)
                total = jnp.where(shift == kh - 1, dot(taps, spread_c), total)
                if kh != 1:
                    edge = 0 if kh == 0 else HGT - 1
                    sides.append(jnp.where(h_of == edge, taps.astype(F32), 0.0))
            at = kd * 3 + kw
            band[:, at * 256 : (at + 1) * 256] = total.astype(BF16)
            band_h[:, at * 64 : (at + 1) * 64] = jnp.concatenate(sides, axis=1).astype(BF16)

    def all_tiles(ref, send, recv):
        span = ref.at[pl.ds(1, ROWS - 1)]
        return pltpu.make_async_remote_copy(
            src_ref=span, dst_ref=span, send_sem=send, recv_sem=recv,
            device_id=device(peer(PEERS[0]), col), device_id_type=MESH,
        )

    all_tiles(tiles.at[1], a_send, a_recv).wait_recv()

    halo_sends = []
    for i, (start, size) in enumerate((((1 - row_z) * 15, 17), (row_z * 17, 15))):
        span = pl.ds(1 + start, size)
        halo_sends.append(
            [
                Shift(tiles.at[1, span], tiles.at[1 - dc, span], h_send.at[i, s], h_recv.at[i, s], 0, dc)
                for s, dc in enumerate((-1, 1))
            ]
        )
    for pair in halo_sends:
        for copy in pair:
            copy.start()

    own_weight.wait()
    for copy in weight_sends:
        copy.wait()

    def patches(heights, start):
        return jnp.concatenate(
            [tiles[b, pl.ds(start + a, 16)].reshape(256, 128) for a in range(3) for b in heights], axis=1
        )

    def taps_of(heights):
        return jnp.concatenate(
            [
                jnp.concatenate([wg[a * 9 + b * 3 + c] for a in range(3) for b in heights], axis=0)
                for c in range(3)
            ],
            axis=1,
        )

    starts = ((1 - row_z) * 16, row_z * 16)
    inner_taps = taps_of((1,))
    inner = [dot(patches((1,), start), inner_taps) for start in starts]
    w_of = iota((256, 128), 0) % WB
    for dz, start in ((1, starts[0]), (0, starts[1])):
        for copy in halo_sends[1 - dz]:
            copy.wait()
        partial = inner[1 - dz] + dot(patches((0, 2), start), taps_of((0, 2)))
        before = pltpu.roll(partial[:, :128], 1, 0)
        after = pltpu.roll(partial[:, 256:], 255, 0)
        summed = partial[:, 128:256] + jnp.where(w_of == 0, 0.0, before) + jnp.where(w_of == WB - 1, 0.0, after)
        part[pl.ds(start, 16)] = summed.astype(BF16).reshape(16, WB, 128)
        for offset in PEERS:
            if offset[0] == dz:
                to = peer(offset)
                pltpu.make_async_remote_copy(
                    src_ref=part.at[to],
                    dst_ref=arrived.at[row],
                    send_sem=p_send,
                    recv_sem=p_recv,
                    device_id=device(to, col),
                    device_id_type=MESH,
                ).start()

    arrived[row] = part[row]
    r_, c_ = iota((512, WB), 0), iota((512, WB), 1)
    spread_w = ones_where((((r_ % WIDTH) // 8) == c_) & ((((r_ % WIDTH) // 2) % 4) == (r_ // WIDTH)))
    r_, c_ = iota((256, 128), 0), iota((256, 128), 1)
    raise_h = ones_where(((c_ % C1) == (r_ // HGT)) & ((c_ // C1) == (r_ % HGT) // 2))
    loads[3].wait()
    all_tiles(arrived, p_send, p_recv).wait_recv()

    groups = arrived[...].reshape(ROWS // GROUP, GROUP, WB, 128).astype(F32).sum(axis=0)
    middle = silu(jnp.concatenate([groups[k] for k in range(GROUP)], axis=1)).astype(BF16)
    spread = dot(spread_w, middle).astype(BF16)
    raised = jnp.zeros((512, WIDTH), F32)
    for c in range(4):
        raised += dot_nt(up[:, c].reshape(512, CB), spread[c * WIDTH : (c + 1) * WIDTH])

    odd = (iota((64, WIDTH), 1) % 2) == 1
    joined_sends = []
    for i, (first, dr) in enumerate(((0, -1), (384, 1))):
        raised_out[i] = jnp.where(odd, raised[first + 64 : first + 128], raised[first : first + 64]).astype(BF16)
        joined_sends.append(Shift(raised_out.at[i], raised_in.at[1 - i], j_send.at[i], j_recv.at[i], dr, 0))
        joined_sends[-1].start()
    raised = raised.astype(BF16)

    v_of = iota((256, WIDTH), 1)

    def shifted(value):
        v_ = v_of[: value.shape[0]]
        value = value.astype(F32)
        return (
            jnp.where(v_ == 0, 0.0, pltpu.roll(value, 1, 1)).astype(BF16),
            jnp.where(v_ == WIDTH - 1, 0.0, pltpu.roll(value, WIDTH - 1, 1)).astype(BF16),
        )

    r_, c_ = iota((64, 256), 0), iota((64, 256), 1)
    pick = ones_where(((c_ // HGT) == (r_ % C1)) & ((c_ % HGT) == (r_ // C1) * (HGT - 1)))
    lifts = [dot(raise_h, raised[a * 128 : (a + 1) * 128]) for a in range(4)]
    for d in (0, DEP - 1, *range(1, DEP - 1)):
        joined = (feat[d].astype(F32) + lifts[d // 2]).astype(BF16)
        slabs[1 + d, 1] = joined
        rim = dot(pick, joined).astype(BF16)
        edges_out[0, d] = rim[:C1]
        edges_out[1, d] = rim[C1:]
        if d in (0, DEP - 1):
            dr, slot = (-1, DEP + 1) if d == 0 else (1, 0)
            for side, dc in ((0, -1), (1, 1)):
                i = len(joined_sends)
                joined_sends.append(
                    Shift(edges_out.at[side, d], edges_in.at[1 - side, slot], j_send.at[i], j_recv.at[i], dr, dc)
                )
                joined_sends[-1].start()
    for side, dc in ((0, -1), (1, 1)):
        i = len(joined_sends)
        joined_sends.append(
            Shift(edges_out.at[side], edges_in.at[1 - side, pl.ds(1, DEP)], j_send.at[i], j_recv.at[i], 0, dc)
        )
        joined_sends[-1].start()

    for d in range(1, DEP + 1):
        slabs[d, 0], slabs[d, 2] = shifted(slabs[d, 1])
    for d in range(DEP):
        first, last = max(d, 1), min(d + 3, DEP + 1)
        accs[d] = dot(
            band[:, (first - d) * 768 : (last - d) * 768],
            slabs[first:last].reshape((last - first) * 768, WIDTH),
        )

    for copy in feat_sends + joined_sends:
        copy.wait()
    for side in range(2):
        both = raised_in[side].astype(F32)
        even_rows = jnp.where(odd, pltpu.roll(both, 1, 1), both)
        odd_rows = jnp.where(odd, both, pltpu.roll(both, WIDTH - 1, 1))
        lift = dot(raise_h, jnp.concatenate([even_rows, odd_rows], axis=0).astype(BF16))
        d = side * (DEP + 1)
        joined = (feat_in[side].astype(F32) + lift).astype(BF16)
        slabs[d, 1] = joined
        slabs[d, 0], slabs[d, 2] = shifted(joined)
    for d in range(DEP + 2):
        rim = jnp.concatenate([edges_in[0, d], edges_in[1, d]], axis=0)
        edges[d, 1] = rim
        edges[d, 0], edges[d, 2] = shifted(rim)
    for d in range(DEP):
        total = accs[d]
        if d == 0:
            total += dot(band[:, :768], slabs[0].reshape(768, WIDTH))
        if d == DEP - 1:
            total += dot(band[:, 1536:], slabs[DEP + 1].reshape(768, WIDTH))
        total += dot(band_h[...], edges[d : d + 3].reshape(9 * 64, WIDTH))
        out_ref[d] = silu(total).astype(BF16)

    all_tiles(tiles.at[1], a_send, a_recv).wait_send()
    all_tiles(arrived, p_send, p_recv).wait_send()


def body(features, down_weight, bott_weight, up_weight, dec_weight):
    dma = pltpu.SemaphoreType.DMA
    out = pl.pallas_call(
        kernel,
        out_shape=jax.ShapeDtypeStruct((DEP, 256, WIDTH), BF16),
        in_specs=[pl.BlockSpec(memory_space=pltpu.HBM)] * 5,
        out_specs=pl.BlockSpec(memory_space=pltpu.VMEM),
        scratch_shapes=[
            pltpu.VMEM((DEP, 256, WIDTH), BF16),
            pltpu.VMEM((16, 4, C1, CB), BF16),
            pltpu.VMEM((16, 4, C1, CB), BF16),
            pltpu.VMEM((27, C1, C1), BF16),
            pltpu.VMEM((27, 128, 128), BF16),
            pltpu.VMEM((4, WB, 128), BF16),
            pltpu.VMEM((3, ROWS + 2, WB, 128), BF16),
            pltpu.VMEM((ROWS, WB, 128), BF16),
            pltpu.VMEM((ROWS, WB, 128), BF16),
            pltpu.VMEM((256, 9 * 256), BF16),
            pltpu.VMEM((256, 9 * 64), BF16),
            pltpu.VMEM((DEP + 2, 3, 256, WIDTH), BF16),
            pltpu.VMEM((2, DEP, C1, WIDTH), BF16),
            pltpu.VMEM((2, DEP + 2, C1, WIDTH), BF16),
            pltpu.VMEM((DEP + 2, 3, 64, WIDTH), BF16),
            pltpu.VMEM((DEP, 256, WIDTH), F32),
            pltpu.VMEM((2, 256, WIDTH), BF16),
            pltpu.VMEM((2, 64, WIDTH), BF16),
            pltpu.VMEM((2, 64, WIDTH), BF16),
            dma((5,)), dma((3,)), dma((3,)), dma, dma, dma((2, 2)), dma((2, 2)), dma, dma, dma((8,)), dma((8,)),
            dma((2,)), dma((2,)),
        ],
        compiler_params=pltpu.CompilerParams(
            collective_id=0, has_side_effects=True, vmem_limit_bytes=60 * 1024 * 1024
        ),
        name="encode_decode",
    )(
        features.reshape(DEP, 256, WIDTH),
        down_weight.reshape(16, 4, C1, CB),
        bott_weight.reshape(27, CIN, CB),
        up_weight.reshape(16, 4, C1, CB),
        dec_weight.reshape(27, C1, C1),
    )
    return out.reshape(features.shape)


def solution(mesh):
    placed = (P("row", None, "col", None), P(), P(None, None, None, "row", None), P(), P())
    return jax.shard_map(
        body, mesh=mesh, in_specs=placed, out_specs=P("row", None, "col", None), check_vma=False
    )
```

time: 58.2 us -> 41.4 us (0.71)
  Pallas kernels: 51 us -> 39.4 us
  local copies, waits for them, and re-layouts: 6.97 us -> 1.87 us
    pallas_call x1, Pallas kernels: 51 us -> 39.4 us  [body(): pl.pallas_call(kernel, out_shape=jax.ShapeDtypeStruct((DEP, 256, WIDTH),...]
    unnamed x11 -> x1, local copies, waits for them, and re-layouts: 6.97 us -> 1.87 us
where the time goes in v2:
time: 41.4 us; the launch traced here: 41.3 us
  Pallas kernels  39.4 us (95%)
  local copies, waits for them, and re-layouts  1.87 us (5%)
    pallas_call x1, Pallas kernels, body(): pl.pallas_call(kernel, out_shape=jax.ShapeDtypeStruct((DEP, 256, WIDTH),...  39.4 us
    unnamed x1, local copies, waits for them, and re-layouts  1.87 us

profile of v2, /device:TPU:1, one launch (start us, length us, event | category | flops | bytes accessed | tf_op | source)
XLA Modules:
  0.0 41.3 jit_solution(3712944780518171119)
XLA Ops:
  0.0 39.4 %encode_decode.1 = bf16[8,256,128]{2,1,0:T(8,128)(2,1)} custom-call(bf16[8,256,128]{2,1,0:T(8,128)(2,1)} %bitcast.9, bf16[16,4,32,512]{3,2,1,0:T(8,128)(2,1)} %bitcast.7, bf16[27,16,512]{2,1,0:T(8,128)(2,1)} %bitcast.10, bf16[16,4,32,512]{3,2,1,0:T(8,128)(2,1)} %bitcast.8, bf16[27,32,32]{2,1,0:T(8,128)(2,1)} %bitcast.11), custom_call_target="tpu_custom_call" | custom-call | tf_op jit(solution)/shard_map/encode_decode/pallas_call | solution.py:382
  39.4 1.9 %copy.7 = bf16[8,32,8,128]{3,2,1,0:T(8,128)(2,1)} copy(bf16[8,32,8,128]{3,2,1,0:T(8,128)(2,1)} %bitcast.6) | data formatting | bytes 1048576

commit v3 on v2

--- a/solution.py
+++ b/solution.py
@@ -12,6 +12,7 @@
 C1, CB, WIDTH = 32, 512, 128
 DEP, HGT, WB = 8, 8, 16
 CIN = CB // ROWS
+SEAM = ROWS // 2
 NT = (((1,), (1,)), ((), ()))
 
 
@@ -50,8 +51,10 @@
 def kernel(
     feat_hbm, down_hbm, bott_hbm, up_hbm, dec_hbm, out_ref,
     feat, down, up, dec, wg, lowered, tiles, part, arrived, band, band_h,
-    slabs, edges_out, edges_in, edges, accs, feat_in, raised_out, raised_in,
-    load_sem, w_send, w_recv, a_send, a_recv, h_send, h_recv, p_send, p_recv, j_send, j_recv, f_send, f_recv,
+    slabs, edges, accs, feat_in, feat_rim, feat_rim_in, beyond,
+    raised_out, raised_in, rim_out, rim_in, corner_out, corner_in,
+    load_sem, w_send, w_recv, a_send, a_recv, h_send, h_recv, p_send, p_recv, b_send, b_recv,
+    j_send, j_recv, f_send, f_recv, s_send, s_recv,
 ):
     row, col = lax.axis_index("row"), lax.axis_index("col")
     row_z, row_x, lane = row // 16, (row // GROUP) % 4, row % GROUP
@@ -63,25 +66,6 @@
     def peer(offset):
         dz, dx, dy = offset
         return (row_z + dz) % 2 * 16 + (row_x + dx) % 4 * GROUP + (lane + dy) % GROUP
-
-    loads = [
-        pltpu.make_async_copy(src, dst, load_sem.at[i])
-        for i, (src, dst) in enumerate(
-            [(feat_hbm, feat), (down_hbm, down), (dec_hbm, dec), (up_hbm, up)]
-        )
-    ]
-    for load in loads:
-        load.start()
-
-    def weight_slot(owner_lane):
-        start = pl.multiple_of(half * (GROUP * CIN) + owner_lane * CIN, CIN)
-        return wg.at[:, pl.ds(start, CIN), :]
-
-    def weight_piece(lane_to):
-        return bott_hbm.at[:, :, pl.ds(pl.multiple_of(lane_to * 128, 128), 128)]
-
-    own_weight = pltpu.make_async_copy(weight_piece(lane), weight_slot(lane), load_sem.at[4])
-    own_weight.start()
 
     barrier = pltpu.get_barrier_semaphore()
 
@@ -94,6 +78,25 @@
         for dc in (-1, 1):
             greet((row + dr + ROWS) % ROWS, (col + dc + COLS) % COLS)
 
+    loads = [
+        pltpu.make_async_copy(src, dst, load_sem.at[i])
+        for i, (src, dst) in enumerate(
+            [(feat_hbm, feat), (down_hbm, down), (dec_hbm, dec), (up_hbm, up)]
+        )
+    ]
+    for load in loads:
+        load.start()
+
+    def weight_slot(owner_lane):
+        start = pl.multiple_of(half * (GROUP * CIN) + owner_lane * CIN, CIN)
+        return wg.at[:, pl.ds(start, CIN), :]
+
+    def weight_piece(lane_to):
+        return bott_hbm.at[:, :, pl.ds(pl.multiple_of(lane_to * 128, 128), 128)]
+
+    own_weight = pltpu.make_async_copy(weight_piece(lane), weight_slot(lane), load_sem.at[4])
+    own_weight.start()
+
     rest = pl.multiple_of((1 - half) * (GROUP * CIN), GROUP * CIN)
     wg[:, pl.ds(rest, GROUP * CIN), :] = jnp.zeros((27, GROUP * CIN, 128), BF16)
     tiles[:, 0] = jnp.zeros((3, WB, 128), BF16)
@@ -104,13 +107,16 @@
         def _():
             feat_in[side] = jnp.zeros((256, WIDTH), BF16)
             raised_in[side] = jnp.zeros((64, WIDTH), BF16)
-            edges_in[:, side * (DEP + 1)] = jnp.zeros((2, C1, WIDTH), BF16)
+            feat_rim_in[:, side * (DEP + 1)] = jnp.zeros((2, C1, WIDTH), BF16)
+            corner_in[:, side] = jnp.zeros((2, C1, WIDTH), BF16)
 
     for side, edge in ((0, col == 0), (1, col == COLS - 1)):
         @pl.when(edge)
         def _():
             tiles[2 * side] = jnp.zeros((ROWS + 2, WB, 128), BF16)
-            edges_in[side] = jnp.zeros((DEP + 2, C1, WIDTH), BF16)
+            feat_rim_in[side] = jnp.zeros((DEP + 2, C1, WIDTH), BF16)
+            rim_in[side] = jnp.zeros((64, WIDTH), BF16)
+            corner_in[side] = jnp.zeros((2, C1, WIDTH), BF16)
 
     def inside(dr, dc):
         yes = None
@@ -120,25 +126,31 @@
                 yes = here if yes is None else jnp.logical_and(yes, here)
         return yes
 
+    def off_seam(dr):
+        return row != SEAM - 1 if dr > 0 else row != SEAM
+
     class Shift:
-        def __init__(self, src, dst, send, recv, dr, dc):
-            self.there, self.back = (dr, dc), (-dr, -dc)
+        def __init__(self, src, dst, send, recv, dr, dc, seam=None):
+            self.there, self.back = inside(dr, dc), inside(-dr, -dc)
+            if seam is not None:
+                self.there = jnp.logical_and(self.there, off_seam(dr))
+                self.back = jnp.logical_and(self.back, off_seam(-dr))
             self.copy = pltpu.make_async_remote_copy(
                 src_ref=src, dst_ref=dst, send_sem=send, recv_sem=recv,
                 device_id=device((row + dr + ROWS) % ROWS, (col + dc + COLS) % COLS), device_id_type=MESH,
             )
 
         def start(self):
-            @pl.when(inside(*self.there))
+            @pl.when(self.there)
             def _():
                 self.copy.start()
 
         def wait(self):
-            @pl.when(inside(*self.there))
+            @pl.when(self.there)
             def _():
                 self.copy.wait_send()
 
-            @pl.when(inside(*self.back))
+            @pl.when(self.back)
             def _():
                 self.copy.wait_recv()
 
@@ -162,6 +174,13 @@
     for k in range(4):
         lowered[k] = low[:, k * 128 : (k + 1) * 128]
 
+    r_, c_ = iota((64, 256), 0), iota((64, 256), 1)
+    pick = ones_where(((c_ // HGT) == (r_ % C1)) & ((c_ % HGT) == (r_ // C1) * (HGT - 1)))
+    for d in range(DEP):
+        rim = dot(pick, feat[d]).astype(BF16)
+        feat_rim[0, d] = rim[:C1]
+        feat_rim[1, d] = rim[C1:]
+
     pl.semaphore_wait(barrier, ROWS - 1 + 6)
 
     for offset in PEERS:
@@ -189,9 +208,14 @@
         copy.start()
         weight_sends.append(copy)
 
+    sides, ends = ((0, -1), (1, 1)), ((0, -1, 0), (1, 1, DEP - 1))
+    feat_moves = [(feat.at[d], feat_in.at[1 - e], dr, 0) for e, dr, d in ends]
+    feat_moves += [(feat_rim.at[s], feat_rim_in.at[1 - s, pl.ds(1, DEP)], 0, dc) for s, dc in sides]
+    feat_moves += [
+        (feat_rim.at[s, d], feat_rim_in.at[1 - s, (1 - e) * (DEP + 1)], dr, dc) for s, dc in sides for e, dr, d in ends
+    ]
     feat_sends = [
-        Shift(feat.at[0], feat_in.at[1], f_send.at[0], f_recv.at[0], -1, 0),
-        Shift(feat.at[DEP - 1], feat_in.at[0], f_send.at[1], f_recv.at[1], 1, 0),
+        Shift(src, dst, f_send.at[i], f_recv.at[i], dr, dc) for i, (src, dst, dr, dc) in enumerate(feat_moves)
     ]
     for copy in feat_sends:
         copy.start()
@@ -208,16 +232,16 @@
     for kd in range(3):
         for kw in range(3):
             total = jnp.zeros((256, 256), F32)
-            sides = []
+            tops = []
             for kh in range(3):
                 taps = dot_nt(spread_o, dec[(kd * 3 + kh) * 3 + kw]).astype(BF16)
                 total = jnp.where(shift == kh - 1, dot(taps, spread_c), total)
                 if kh != 1:
                     edge = 0 if kh == 0 else HGT - 1
-                    sides.append(jnp.where(h_of == edge, taps.astype(F32), 0.0))
+                    tops.append(jnp.where(h_of == edge, taps.astype(F32), 0.0))
             at = kd * 3 + kw
             band[:, at * 256 : (at + 1) * 256] = total.astype(BF16)
-            band_h[:, at * 64 : (at + 1) * 64] = jnp.concatenate(sides, axis=1).astype(BF16)
+            band_h[:, at * 64 : (at + 1) * 64] = jnp.concatenate(tops, axis=1).astype(BF16)
 
     def all_tiles(ref, send, recv):
         span = ref.at[pl.ds(1, ROWS - 1)]
@@ -257,6 +281,12 @@
                 for c in range(3)
             ],
             axis=1,
+        )
+
+    def beyond_copy(i, to):
+        return pltpu.make_async_remote_copy(
+            src_ref=part.at[2 * SEAM - 1 - to], dst_ref=beyond.at[row],
+            send_sem=b_send.at[i], recv_sem=b_recv, device_id=device(to, col), device_id_type=MESH,
         )
 
     starts = ((1 - row_z) * 16, row_z * 16)
@@ -271,6 +301,16 @@
         after = pltpu.roll(partial[:, 256:], 255, 0)
         summed = partial[:, 128:256] + jnp.where(w_of == 0, 0.0, before) + jnp.where(w_of == WB - 1, 0.0, after)
         part[pl.ds(start, 16)] = summed.astype(BF16).reshape(16, WB, 128)
+        if dz == 0:
+            for i, to in enumerate((SEAM, SEAM - 1)):
+                @pl.when(row != to)
+                def _():
+                    beyond_copy(i, to).start()
+
+                @pl.when(row == to)
+                def _():
+                    beyond[row] = part[2 * SEAM - 1 - to]
+
         for offset in PEERS:
             if offset[0] == dz:
                 to = peer(offset)
@@ -291,20 +331,71 @@
     loads[3].wait()
     all_tiles(arrived, p_send, p_recv).wait_recv()
 
-    groups = arrived[...].reshape(ROWS // GROUP, GROUP, WB, 128).astype(F32).sum(axis=0)
-    middle = silu(jnp.concatenate([groups[k] for k in range(GROUP)], axis=1)).astype(BF16)
-    spread = dot(spread_w, middle).astype(BF16)
-    raised = jnp.zeros((512, WIDTH), F32)
-    for c in range(4):
-        raised += dot_nt(up[:, c].reshape(512, CB), spread[c * WIDTH : (c + 1) * WIDTH])
+    def spread_of(shares):
+        groups = shares.reshape(ROWS // GROUP, GROUP, WB, 128).astype(F32).sum(axis=0)
+        middle = silu(jnp.concatenate([groups[k] for k in range(GROUP)], axis=1)).astype(BF16)
+        return dot(spread_w, middle).astype(BF16)
+
+    def raised_layer(a, spread):
+        total = jnp.zeros((128, WIDTH), F32)
+        for c in range(4):
+            total += dot_nt(up[pl.ds(a * 4, 4), c].reshape(128, CB), spread[c * WIDTH : (c + 1) * WIDTH])
+        return total
 
     odd = (iota((64, WIDTH), 1) % 2) == 1
+
+    def packed(value):
+        return jnp.where(odd, value[64:], value[:64]).astype(BF16)
+
+    def unpacked(value):
+        both = value.astype(F32)
+        even_rows = jnp.where(odd, pltpu.roll(both, 1, 1), both)
+        odd_rows = jnp.where(odd, both, pltpu.roll(both, WIDTH - 1, 1))
+        return jnp.concatenate([even_rows, odd_rows], axis=0)
+
+    spread = spread_of(arrived[...])
+    raised = [None] * 4
     joined_sends = []
-    for i, (first, dr) in enumerate(((0, -1), (384, 1))):
-        raised_out[i] = jnp.where(odd, raised[first + 64 : first + 128], raised[first : first + 64]).astype(BF16)
-        joined_sends.append(Shift(raised_out.at[i], raised_in.at[1 - i], j_send.at[i], j_recv.at[i], dr, 0))
+
+    def send(src, dst, dr, dc, seam=None):
+        i = len(joined_sends)
+        joined_sends.append(Shift(src, dst, j_send.at[i], j_recv.at[i], dr, dc, seam))
         joined_sends[-1].start()
-    raised = raised.astype(BF16)
+
+    for e, dr, a in ((0, -1, 0), (1, 1, 3)):
+        raised[a] = raised_layer(a, spread)
+        raised_out[e] = packed(raised[a])
+        send(raised_out.at[e], raised_in.at[1 - e], dr, 0, False)
+        for s, dc in sides:
+            corner_out[s, e] = raised[a][96 * s : 96 * s + C1].astype(BF16)
+            send(corner_out.at[s, e], corner_in.at[1 - s, 1 - e], dr, dc, False)
+    for a in (1, 2):
+        raised[a] = raised_layer(a, spread)
+    for s, dc in sides:
+        rim_out[s] = packed(jnp.concatenate([raised[a][96 * s : 96 * s + C1] for a in range(4)], axis=0))
+        send(rim_out.at[s], rim_in.at[1 - s], 0, dc)
+
+    for copy in feat_sends:
+        copy.wait()
+
+    for e, here, dr in ((0, SEAM, -1), (1, SEAM - 1, 1)):
+        @pl.when(row == here)
+        def _():
+            all_tiles(beyond, b_send.at[0], b_recv).wait_recv()
+            layer = raised_layer(3 * (1 - e), spread_of(beyond[...]))
+            raised_in[e] = packed(layer)
+            for s in range(2):
+                corner_out[s, 2 + e] = layer[96 * s : 96 * s + C1].astype(BF16)
+
+    for e, here in ((0, SEAM), (1, SEAM - 1)):
+        for s, dc in sides:
+            copy = Shift(
+                corner_out.at[s, 2 + e], corner_in.at[1 - s, e], s_send.at[s, e], s_recv.at[s, e], 0, dc
+            )
+            copy.there = jnp.logical_and(copy.there, row == here)
+            copy.back = jnp.logical_and(copy.back, row == here)
+            copy.start()
+            joined_sends.append(copy)
 
     v_of = iota((256, WIDTH), 1)
 
@@ -316,65 +407,58 @@
             jnp.where(v_ == WIDTH - 1, 0.0, pltpu.roll(value, WIDTH - 1, 1)).astype(BF16),
         )
 
-    r_, c_ = iota((64, 256), 0), iota((64, 256), 1)
-    pick = ones_where(((c_ // HGT) == (r_ % C1)) & ((c_ % HGT) == (r_ // C1) * (HGT - 1)))
-    lifts = [dot(raise_h, raised[a * 128 : (a + 1) * 128]) for a in range(4)]
-    for d in (0, DEP - 1, *range(1, DEP - 1)):
-        joined = (feat[d].astype(F32) + lifts[d // 2]).astype(BF16)
-        slabs[1 + d, 1] = joined
-        rim = dot(pick, joined).astype(BF16)
-        edges_out[0, d] = rim[:C1]
-        edges_out[1, d] = rim[C1:]
-        if d in (0, DEP - 1):
-            dr, slot = (-1, DEP + 1) if d == 0 else (1, 0)
-            for side, dc in ((0, -1), (1, 1)):
-                i = len(joined_sends)
-                joined_sends.append(
-                    Shift(edges_out.at[side, d], edges_in.at[1 - side, slot], j_send.at[i], j_recv.at[i], dr, dc)
-                )
-                joined_sends[-1].start()
-    for side, dc in ((0, -1), (1, 1)):
-        i = len(joined_sends)
-        joined_sends.append(
-            Shift(edges_out.at[side], edges_in.at[1 - side, pl.ds(1, DEP)], j_send.at[i], j_recv.at[i], 0, dc)
-        )
-        joined_sends[-1].start()
-
-    for d in range(1, DEP + 1):
-        slabs[d, 0], slabs[d, 2] = shifted(slabs[d, 1])
+    def store_slab(i, layer, lift):
+        joined = layer.astype(F32) + lift
+        slabs[i, 1] = joined.astype(BF16)
+        slabs[i, 0], slabs[i, 2] = shifted(joined.astype(BF16))
+
     for d in range(DEP):
-        first, last = max(d, 1), min(d + 3, DEP + 1)
-        accs[d] = dot(
-            band[:, (first - d) * 768 : (last - d) * 768],
-            slabs[first:last].reshape((last - first) * 768, WIDTH),
-        )
-
-    for copy in feat_sends + joined_sends:
+        if d % 2 == 0:
+            lift = dot(raise_h, raised[d // 2].astype(BF16))
+        store_slab(1 + d, feat[d], lift)
+
+    def windows(ref, d, first, last, size):
+        return jnp.concatenate(
+            [ref[d + i + first : d + i + last].reshape((last - first) * 3 * size, WIDTH) for i in range(2)], axis=1
+        )
+
+    spans = ((1, 3), (0, 3), (0, 3), (0, 2))
+    for p, (first, last) in enumerate(spans):
+        accs[p] = dot(band[:, first * 768 : last * 768], windows(slabs, 2 * p, first, last, 256))
+
+    for copy in joined_sends:
         copy.wait()
-    for side in range(2):
-        both = raised_in[side].astype(F32)
-        even_rows = jnp.where(odd, pltpu.roll(both, 1, 1), both)
-        odd_rows = jnp.where(odd, both, pltpu.roll(both, WIDTH - 1, 1))
-        lift = dot(raise_h, jnp.concatenate([even_rows, odd_rows], axis=0).astype(BF16))
-        d = side * (DEP + 1)
-        joined = (feat_in[side].astype(F32) + lift).astype(BF16)
-        slabs[d, 1] = joined
-        slabs[d, 0], slabs[d, 2] = shifted(joined)
+    for e in range(2):
+        store_slab(e * (DEP + 1), feat_in[e], dot(raise_h, unpacked(raised_in[e]).astype(BF16)))
+    rims = [unpacked(rim_in[s]) for s in range(2)]
     for d in range(DEP + 2):
-        rim = jnp.concatenate([edges_in[0, d], edges_in[1, d]], axis=0)
+        rim = []
+        for s in range(2):
+            if d in (0, DEP + 1):
+                lift = corner_in[s, d // (DEP + 1)].astype(F32)
+            else:
+                a = (d - 1) // 2
+                lift = rims[s][a * C1 : (a + 1) * C1]
+            rim.append((feat_rim_in[s, d].astype(F32) + lift).astype(BF16))
+        rim = jnp.concatenate(rim, axis=0)
         edges[d, 1] = rim
         edges[d, 0], edges[d, 2] = shifted(rim)
-    for d in range(DEP):
-        total = accs[d]
-        if d == 0:
-            total += dot(band[:, :768], slabs[0].reshape(768, WIDTH))
-        if d == DEP - 1:
-            total += dot(band[:, 1536:], slabs[DEP + 1].reshape(768, WIDTH))
-        total += dot(band_h[...], edges[d : d + 3].reshape(9 * 64, WIDTH))
-        out_ref[d] = silu(total).astype(BF16)
+    for p in range(4):
+        total = accs[p] + dot(band_h[...], windows(edges, 2 * p, 0, 3, 64))
+        if p == 0:
+            total += dot(band[:, :768], windows(slabs, 0, 0, 1, 256))
+        if p == 3:
+            total += dot(band[:, 1536:], windows(slabs, 6, 2, 3, 256))
+        total = silu(total).astype(BF16)
+        out_ref[2 * p] = total[:, :WIDTH]
+        out_ref[2 * p + 1] = total[:, WIDTH:]
 
     all_tiles(tiles.at[1], a_send, a_recv).wait_send()
     all_tiles(arrived, p_send, p_recv).wait_send()
+    for i, to in enumerate((SEAM, SEAM - 1)):
+        @pl.when(row != to)
+        def _():
+            beyond_copy(i, to).wait_send()
 
 
 def body(features, down_weight, bott_weight, up_weight, dec_weight):
@@ -397,15 +481,20 @@
             pltpu.VMEM((256, 9 * 256), BF16),
             pltpu.VMEM((256, 9 * 64), BF16),
             pltpu.VMEM((DEP + 2, 3, 256, WIDTH), BF16),
+            pltpu.VMEM((DEP + 2, 3, 64, WIDTH), BF16),
+            pltpu.VMEM((DEP // 2, 256, 2 * WIDTH), F32),
+            pltpu.VMEM((2, 256, WIDTH), BF16),
             pltpu.VMEM((2, DEP, C1, WIDTH), BF16),
             pltpu.VMEM((2, DEP + 2, C1, WIDTH), BF16),
-            pltpu.VMEM((DEP + 2, 3, 64, WIDTH), BF16),
-            pltpu.VMEM((DEP, 256, WIDTH), F32),
-            pltpu.VMEM((2, 256, WIDTH), BF16),
+            pltpu.VMEM((ROWS, WB, 128), BF16),
             pltpu.VMEM((2, 64, WIDTH), BF16),
             pltpu.VMEM((2, 64, WIDTH), BF16),
-            dma((5,)), dma((3,)), dma((3,)), dma, dma, dma((2, 2)), dma((2, 2)), dma, dma, dma((8,)), dma((8,)),
-            dma((2,)), dma((2,)),
+            pltpu.VMEM((2, 64, WIDTH), BF16),
+            pltpu.VMEM((2, 64, WIDTH), BF16),
+            pltpu.VMEM((2, 4, C1, WIDTH), BF16),
+            pltpu.VMEM((2, 2, C1, WIDTH), BF16),
+            dma((5,)), dma((3,)), dma((3,)), dma, dma, dma((2, 2)), dma((2, 2)), dma, dma, dma((2,)), dma,
+            dma((8,)), dma((8,)), dma((8,)), dma((8,)), dma((2, 2)), dma((2, 2)),
         ],
         compiler_params=pltpu.CompilerParams(
             collective_id=0, has_side_effects=True, vmem_limit_bytes=60 * 1024 * 1024

time: 41.4 us -> 39.1 us (0.944)
  Pallas kernels: 39.4 us -> 36.9 us
    pallas_call x1, Pallas kernels: 39.4 us -> 36.9 us  [body(): pl.pallas_call(kernel, out_shape=jax.ShapeDtypeStruct((DEP, 256, WIDTH),...]
where the time goes in v3:
time: 39.1 us; the launch traced here: 38.8 us
  Pallas kernels  36.9 us (94%)
  local copies, waits for them, and re-layouts  1.87 us (5%)
    pallas_call x1, Pallas kernels, body(): pl.pallas_call(kernel, out_shape=jax.ShapeDtypeStruct((DEP, 256, WIDTH),...  36.9 us
    unnamed x1, local copies, waits for them, and re-layouts  1.87 us

profile of v3, /device:TPU:1, one launch (start us, length us, event | category | flops | bytes accessed | tf_op | source)
XLA Modules:
  0.0 38.8 jit_solution(1694404740718428971)
XLA Ops:
  0.0 36.9 %encode_decode.1 = bf16[8,256,128]{2,1,0:T(8,128)(2,1)} custom-call(bf16[8,256,128]{2,1,0:T(8,128)(2,1)} %bitcast.9, bf16[16,4,32,512]{3,2,1,0:T(8,128)(2,1)} %bitcast.7, bf16[27,16,512]{2,1,0:T(8,128)(2,1)} %bitcast.10, bf16[16,4,32,512]{3,2,1,0:T(8,128)(2,1)} %bitcast.8, bf16[27,32,32]{2,1,0:T(8,128)(2,1)} %bitcast.11), custom_call_target="tpu_custom_call" | custom-call | tf_op jit(solution)/shard_map/encode_decode/pallas_call | solution.py:466
  36.9 1.9 %copy.7 = bf16[8,32,8,128]{3,2,1,0:T(8,128)(2,1)} copy(bf16[8,32,8,128]{3,2,1,0:T(8,128)(2,1)} %bitcast.6) | data formatting | bytes 1048576

commit v4 on v3

--- a/solution.py
+++ b/solution.py
@@ -25,7 +25,7 @@
 
 
 def silu(v):
-    return v / (1.0 + jnp.exp(-v))
+    return 0.5 * v * (1.0 + jnp.tanh(0.5 * v))
 
 
 def dot(a, b):
@@ -140,8 +140,8 @@
                 device_id=device((row + dr + ROWS) % ROWS, (col + dc + COLS) % COLS), device_id_type=MESH,
             )
 
-        def start(self):
-            @pl.when(self.there)
+        def start(self, also=None):
+            @pl.when(self.there if also is None else jnp.logical_and(self.there, also))
             def _():
                 self.copy.start()
 
@@ -194,12 +194,17 @@
             device_id_type=MESH,
         ).start()
 
+    core = col % 2
+
+    def taps_at(ref, start, size):
+        return ref.at[pl.ds(start, size)]
+
     weight_sends = []
     for j in range(1, GROUP):
         to = (lane + j) % GROUP
         copy = pltpu.make_async_remote_copy(
-            src_ref=weight_piece(to),
-            dst_ref=weight_slot(lane),
+            src_ref=taps_at(weight_piece(to), core * 13, 14),
+            dst_ref=taps_at(weight_slot(lane), core * 13, 14),
             send_sem=w_send.at[j - 1],
             recv_sem=w_recv.at[j - 1],
             device_id=device(row - lane + to, col),
@@ -207,6 +212,15 @@
         )
         copy.start()
         weight_sends.append(copy)
+    twin_sends = []
+    for j in range(1, GROUP):
+        slot = taps_at(weight_slot((lane + j) % GROUP), core * 14, 13)
+        twin_sends.append(
+            pltpu.make_async_remote_copy(
+                src_ref=slot, dst_ref=slot, send_sem=w_send.at[GROUP + j - 2], recv_sem=w_recv.at[GROUP + j - 2],
+                device_id=device(row, col + 1 - 2 * core), device_id_type=MESH,
+            )
+        )
 
     sides, ends = ((0, -1), (1, 1)), ((0, -1, 0), (1, 1, DEP - 1))
     feat_moves = [(feat.at[d], feat_in.at[1 - e], dr, 0) for e, dr, d in ends]
@@ -217,8 +231,9 @@
     feat_sends = [
         Shift(src, dst, f_send.at[i], f_recv.at[i], dr, dc) for i, (src, dst, dr, dc) in enumerate(feat_moves)
     ]
-    for copy in feat_sends:
-        copy.start()
+    for copy, (_, _, dr, _) in zip(feat_sends, feat_moves):
+        if dr:
+            copy.start(jnp.logical_not(off_seam(dr)))
 
     tiles[1, 1 + row] = lowered[row // 8]
 
@@ -268,6 +283,12 @@
     own_weight.wait()
     for copy in weight_sends:
         copy.wait()
+    for copy in twin_sends:
+        copy.start()
+    for copy, (_, _, dr, _) in zip(feat_sends, feat_moves):
+        copy.start(off_seam(dr) if dr else None)
+    for copy in twin_sends:
+        copy.wait()
 
     def patches(heights, start):
         return jnp.concatenate(
@@ -324,7 +345,7 @@
                 ).start()
 
     arrived[row] = part[row]
-    r_, c_ = iota((512, WB), 0), iota((512, WB), 1)
+    r_, c_ = iota((WB, 512), 1), iota((WB, 512), 0)
     spread_w = ones_where((((r_ % WIDTH) // 8) == c_) & ((((r_ % WIDTH) // 2) % 4) == (r_ // WIDTH)))
     r_, c_ = iota((256, 128), 0), iota((256, 128), 1)
     raise_h = ones_where(((c_ % C1) == (r_ // HGT)) & ((c_ // C1) == (r_ % HGT) // 2))
@@ -334,13 +355,15 @@
     def spread_of(shares):
         groups = shares.reshape(ROWS // GROUP, GROUP, WB, 128).astype(F32).sum(axis=0)
         middle = silu(jnp.concatenate([groups[k] for k in range(GROUP)], axis=1)).astype(BF16)
-        return dot(spread_w, middle).astype(BF16)
-
-    def raised_layer(a, spread):
-        total = jnp.zeros((128, WIDTH), F32)
-        for c in range(4):
-            total += dot_nt(up[pl.ds(a * 4, 4), c].reshape(128, CB), spread[c * WIDTH : (c + 1) * WIDTH])
-        return total
+        across = lax.dot_general(middle, spread_w, (((0,), (0,)), ((), ())), preferred_element_type=F32)
+        across = across.astype(BF16)
+        return jnp.concatenate([across[:, c * WIDTH : (c + 1) * WIDTH] for c in range(4)], axis=0)
+
+    def raised_layers(layers, spread):
+        rows = [
+            jnp.concatenate([up[a * 4 : a * 4 + 4, c].reshape(128, CB) for a in layers], axis=0) for c in range(4)
+        ]
+        return dot(jnp.concatenate(rows, axis=1), spread)
 
     odd = (iota((64, WIDTH), 1) % 2) == 1
 
@@ -362,15 +385,16 @@
         joined_sends.append(Shift(src, dst, j_send.at[i], j_recv.at[i], dr, dc, seam))
         joined_sends[-1].start()
 
+    outer = raised_layers((0, 3), spread)
+    raised[0], raised[3] = outer[:128], outer[128:]
     for e, dr, a in ((0, -1, 0), (1, 1, 3)):
-        raised[a] = raised_layer(a, spread)
         raised_out[e] = packed(raised[a])
         send(raised_out.at[e], raised_in.at[1 - e], dr, 0, False)
         for s, dc in sides:
             corner_out[s, e] = raised[a][96 * s : 96 * s + C1].astype(BF16)
             send(corner_out.at[s, e], corner_in.at[1 - s, 1 - e], dr, dc, False)
-    for a in (1, 2):
-        raised[a] = raised_layer(a, spread)
+    inner = raised_layers((1, 2), spread)
+    raised[1], raised[2] = inner[:128], inner[128:]
     for s, dc in sides:
         rim_out[s] = packed(jnp.concatenate([raised[a][96 * s : 96 * s + C1] for a in range(4)], axis=0))
         send(rim_out.at[s], rim_in.at[1 - s], 0, dc)
@@ -382,7 +406,7 @@
         @pl.when(row == here)
         def _():
             all_tiles(beyond, b_send.at[0], b_recv).wait_recv()
-            layer = raised_layer(3 * (1 - e), spread_of(beyond[...]))
+            layer = raised_layers((3 * (1 - e),), spread_of(beyond[...]))
             raised_in[e] = packed(layer)
             for s in range(2):
                 corner_out[s, 2 + e] = layer[96 * s : 96 * s + C1].astype(BF16)
@@ -493,7 +517,7 @@
             pltpu.VMEM((2, 64, WIDTH), BF16),
             pltpu.VMEM((2, 4, C1, WIDTH), BF16),
             pltpu.VMEM((2, 2, C1, WIDTH), BF16),
-            dma((5,)), dma((3,)), dma((3,)), dma, dma, dma((2, 2)), dma((2, 2)), dma, dma, dma((2,)), dma,
+            dma((5,)), dma((6,)), dma((6,)), dma, dma, dma((2, 2)), dma((2, 2)), dma, dma, dma((2,)), dma,
             dma((8,)), dma((8,)), dma((8,)), dma((8,)), dma((2, 2)), dma((2, 2)),
         ],
         compiler_params=pltpu.CompilerParams(

time: 39.1 us -> 40.7 us (1.041)
  Pallas kernels: 36.9 us -> 38.7 us
    pallas_call x1, Pallas kernels: 36.9 us -> 38.7 us  [body(): pl.pallas_call(kernel, out_shape=jax.ShapeDtypeStruct((DEP, 256, WIDTH),...]
where the time goes in v4:
time: 40.7 us; the launch traced here: 40.5 us
  Pallas kernels  38.7 us (95%)
  local copies, waits for them, and re-layouts  1.87 us (5%)
    pallas_call x1, Pallas kernels, body(): pl.pallas_call(kernel, out_shape=jax.ShapeDtypeStruct((DEP, 256, WIDTH),...  38.7 us
    unnamed x1, local copies, waits for them, and re-layouts  1.87 us

profile of v4, /device:TPU:1, one launch (start us, length us, event | category | flops | bytes accessed | tf_op | source)
XLA Modules:
  0.0 40.5 jit_solution(6351355363705130522)
XLA Ops:
  0.0 38.7 %encode_decode.1 = bf16[8,256,128]{2,1,0:T(8,128)(2,1)} custom-call(bf16[8,256,128]{2,1,0:T(8,128)(2,1)} %bitcast.9, bf16[16,4,32,512]{3,2,1,0:T(8,128)(2,1)} %bitcast.7, bf16[27,16,512]{2,1,0:T(8,128)(2,1)} %bitcast.10, bf16[16,4,32,512]{3,2,1,0:T(8,128)(2,1)} %bitcast.8, bf16[27,32,32]{2,1,0:T(8,128)(2,1)} %bitcast.11), custom_call_target="tpu_custom_call" | custom-call | tf_op jit(solution)/shard_map/encode_decode/pallas_call | solution.py:490
  38.7 1.9 %copy.7 = bf16[8,32,8,128]{3,2,1,0:T(8,128)(2,1)} copy(bf16[8,32,8,128]{3,2,1,0:T(8,128)(2,1)} %bitcast.6) | data formatting | bytes 1048576

commit v5 on v4

--- a/solution.py
+++ b/solution.py
@@ -194,17 +194,12 @@
             device_id_type=MESH,
         ).start()
 
-    core = col % 2
-
-    def taps_at(ref, start, size):
-        return ref.at[pl.ds(start, size)]
-
     weight_sends = []
     for j in range(1, GROUP):
         to = (lane + j) % GROUP
         copy = pltpu.make_async_remote_copy(
-            src_ref=taps_at(weight_piece(to), core * 13, 14),
-            dst_ref=taps_at(weight_slot(lane), core * 13, 14),
+            src_ref=weight_piece(to),
+            dst_ref=weight_slot(lane),
             send_sem=w_send.at[j - 1],
             recv_sem=w_recv.at[j - 1],
             device_id=device(row - lane + to, col),
@@ -212,15 +207,6 @@
         )
         copy.start()
         weight_sends.append(copy)
-    twin_sends = []
-    for j in range(1, GROUP):
-        slot = taps_at(weight_slot((lane + j) % GROUP), core * 14, 13)
-        twin_sends.append(
-            pltpu.make_async_remote_copy(
-                src_ref=slot, dst_ref=slot, send_sem=w_send.at[GROUP + j - 2], recv_sem=w_recv.at[GROUP + j - 2],
-                device_id=device(row, col + 1 - 2 * core), device_id_type=MESH,
-            )
-        )
 
     sides, ends = ((0, -1), (1, 1)), ((0, -1, 0), (1, 1, DEP - 1))
     feat_moves = [(feat.at[d], feat_in.at[1 - e], dr, 0) for e, dr, d in ends]
@@ -231,9 +217,8 @@
     feat_sends = [
         Shift(src, dst, f_send.at[i], f_recv.at[i], dr, dc) for i, (src, dst, dr, dc) in enumerate(feat_moves)
     ]
-    for copy, (_, _, dr, _) in zip(feat_sends, feat_moves):
-        if dr:
-            copy.start(jnp.logical_not(off_seam(dr)))
+    for copy in feat_sends:
+        copy.start()
 
     tiles[1, 1 + row] = lowered[row // 8]
 
@@ -283,12 +268,6 @@
     own_weight.wait()
     for copy in weight_sends:
         copy.wait()
-    for copy in twin_sends:
-        copy.start()
-    for copy, (_, _, dr, _) in zip(feat_sends, feat_moves):
-        copy.start(off_seam(dr) if dr else None)
-    for copy in twin_sends:
-        copy.wait()
 
     def patches(heights, start):
         return jnp.concatenate(
@@ -432,9 +411,9 @@
         )
 
     def store_slab(i, layer, lift):
-        joined = layer.astype(F32) + lift
-        slabs[i, 1] = joined.astype(BF16)
-        slabs[i, 0], slabs[i, 2] = shifted(joined.astype(BF16))
+        joined = (layer.astype(F32) + lift).astype(BF16)
+        slabs[i, 1] = joined
+        slabs[i, 0], slabs[i, 2] = shifted(joined)
 
     for d in range(DEP):
         if d % 2 == 0:
@@ -450,24 +429,13 @@
     for p, (first, last) in enumerate(spans):
         accs[p] = dot(band[:, first * 768 : last * 768], windows(slabs, 2 * p, first, last, 256))
 
-    for copy in joined_sends:
-        copy.wait()
-    for e in range(2):
-        store_slab(e * (DEP + 1), feat_in[e], dot(raise_h, unpacked(raised_in[e]).astype(BF16)))
-    rims = [unpacked(rim_in[s]) for s in range(2)]
-    for d in range(DEP + 2):
-        rim = []
-        for s in range(2):
-            if d in (0, DEP + 1):
-                lift = corner_in[s, d // (DEP + 1)].astype(F32)
-            else:
-                a = (d - 1) // 2
-                lift = rims[s][a * C1 : (a + 1) * C1]
-            rim.append((feat_rim_in[s, d].astype(F32) + lift).astype(BF16))
+    def store_rim(d, lifts):
+        rim = [(feat_rim_in[s, d].astype(F32) + lifts[s]).astype(BF16) for s in range(2)]
         rim = jnp.concatenate(rim, axis=0)
         edges[d, 1] = rim
         edges[d, 0], edges[d, 2] = shifted(rim)
-    for p in range(4):
+
+    def finish(p):
         total = accs[p] + dot(band_h[...], windows(edges, 2 * p, 0, 3, 64))
         if p == 0:
             total += dot(band[:, :768], windows(slabs, 0, 0, 1, 256))
@@ -476,6 +444,23 @@
         total = silu(total).astype(BF16)
         out_ref[2 * p] = total[:, :WIDTH]
         out_ref[2 * p + 1] = total[:, WIDTH:]
+
+    for copy in joined_sends[6:8]:
+        copy.wait()
+    rims = [unpacked(rim_in[s]) for s in range(2)]
+    for d in range(DEP):
+        a = d // 2
+        store_rim(1 + d, [rims[s][a * C1 : (a + 1) * C1] for s in range(2)])
+    for p in (1, 2):
+        finish(p)
+
+    for copy in joined_sends[:6] + joined_sends[8:]:
+        copy.wait()
+    for e in range(2):
+        store_slab(e * (DEP + 1), feat_in[e], dot(raise_h, unpacked(raised_in[e]).astype(BF16)))
+        store_rim(e * (DEP + 1), [corner_in[s, e].astype(F32) for s in range(2)])
+    for p in (0, 3):
+        finish(p)
 
     all_tiles(tiles.at[1], a_send, a_recv).wait_send()
     all_tiles(arrived, p_send, p_recv).wait_send()

time: 40.7 us -> 38.9 us (0.956)
  Pallas kernels: 38.7 us -> 36.9 us
    pallas_call x1, Pallas kernels: 38.7 us -> 36.9 us  [body(): pl.pallas_call(kernel, out_shape=jax.ShapeDtypeStruct((DEP, 256, WIDTH),...]
where the time goes in v5:
time: 38.9 us; the launch traced here: 38.8 us
  Pallas kernels  36.9 us (95%)
  local copies, waits for them, and re-layouts  1.87 us (5%)
    pallas_call x1, Pallas kernels, body(): pl.pallas_call(kernel, out_shape=jax.ShapeDtypeStruct((DEP, 256, WIDTH),...  36.9 us
    unnamed x1, local copies, waits for them, and re-layouts  1.87 us

profile of v5, /device:TPU:1, one launch (start us, length us, event | category | flops | bytes accessed | tf_op | source)
XLA Modules:
  0.0 38.8 jit_solution(17686465221428068470)
XLA Ops:
  0.0 36.9 %encode_decode.1 = bf16[8,256,128]{2,1,0:T(8,128)(2,1)} custom-call(bf16[8,256,128]{2,1,0:T(8,128)(2,1)} %bitcast.9, bf16[16,4,32,512]{3,2,1,0:T(8,128)(2,1)} %bitcast.7, bf16[27,16,512]{2,1,0:T(8,128)(2,1)} %bitcast.10, bf16[16,4,32,512]{3,2,1,0:T(8,128)(2,1)} %bitcast.8, bf16[27,32,32]{2,1,0:T(8,128)(2,1)} %bitcast.11), custom_call_target="tpu_custom_call" | custom-call | tf_op jit(solution)/shard_map/encode_decode/pallas_call | solution.py:475
  36.9 1.9 %copy.7 = bf16[8,32,8,128]{3,2,1,0:T(8,128)(2,1)} copy(bf16[8,32,8,128]{3,2,1,0:T(8,128)(2,1)} %bitcast.6) | data formatting | bytes 1048576

commit v6 on v5

--- a/solution.py
+++ b/solution.py
@@ -189,7 +189,7 @@
             src_ref=lowered.at[to // 8],
             dst_ref=tiles.at[1, 1 + row],
             send_sem=a_send,
-            recv_sem=a_recv,
+            recv_sem=a_recv.at[offset[0]],
             device_id=device(to, col),
             device_id_type=MESH,
         ).start()
@@ -250,19 +250,21 @@
             device_id=device(peer(PEERS[0]), col), device_id_type=MESH,
         )
 
-    all_tiles(tiles.at[1], a_send, a_recv).wait_recv()
-
     halo_sends = []
-    for i, (start, size) in enumerate((((1 - row_z) * 15, 17), (row_z * 17, 15))):
-        span = pl.ds(1 + start, size)
+    for dz in range(2):
+        start = 1 + (row_z + dz) % 2 * SEAM
+        span, come = pl.ds(start, SEAM), tiles.at[1, pl.ds(start, SEAM - 1 + dz)]
+        pltpu.make_async_remote_copy(
+            src_ref=come, dst_ref=come, send_sem=a_send, recv_sem=a_recv.at[dz],
+            device_id=device(peer(PEERS[0]), col), device_id_type=MESH,
+        ).wait_recv()
         halo_sends.append(
             [
-                Shift(tiles.at[1, span], tiles.at[1 - dc, span], h_send.at[i, s], h_recv.at[i, s], 0, dc)
+                Shift(tiles.at[1, span], tiles.at[1 - dc, span], h_send.at[dz, s], h_recv.at[dz, s], 0, dc)
                 for s, dc in enumerate((-1, 1))
             ]
         )
-    for pair in halo_sends:
-        for copy in pair:
+        for copy in halo_sends[dz]:
             copy.start()
 
     own_weight.wait()
@@ -293,9 +295,9 @@
     inner_taps = taps_of((1,))
     inner = [dot(patches((1,), start), inner_taps) for start in starts]
     w_of = iota((256, 128), 0) % WB
+    for copy in halo_sends[0] + halo_sends[1]:
+        copy.wait()
     for dz, start in ((1, starts[0]), (0, starts[1])):
-        for copy in halo_sends[1 - dz]:
-            copy.wait()
         partial = inner[1 - dz] + dot(patches((0, 2), start), taps_of((0, 2)))
         before = pltpu.roll(partial[:, :128], 1, 0)
         after = pltpu.roll(partial[:, 256:], 255, 0)
@@ -462,7 +464,7 @@
     for p in (0, 3):
         finish(p)
 
-    all_tiles(tiles.at[1], a_send, a_recv).wait_send()
+    all_tiles(tiles.at[1], a_send, a_recv.at[0]).wait_send()
     all_tiles(arrived, p_send, p_recv).wait_send()
     for i, to in enumerate((SEAM, SEAM - 1)):
         @pl.when(row != to)
@@ -502,7 +504,7 @@
             pltpu.VMEM((2, 64, WIDTH), BF16),
             pltpu.VMEM((2, 4, C1, WIDTH), BF16),
             pltpu.VMEM((2, 2, C1, WIDTH), BF16),
-            dma((5,)), dma((6,)), dma((6,)), dma, dma, dma((2, 2)), dma((2, 2)), dma, dma, dma((2,)), dma,
+            dma((5,)), dma((6,)), dma((6,)), dma, dma((2,)), dma((2, 2)), dma((2, 2)), dma, dma, dma((2,)), dma,
             dma((8,)), dma((8,)), dma((8,)), dma((8,)), dma((2, 2)), dma((2, 2)),
         ],
         compiler_params=pltpu.CompilerParams(

time: 38.9 us -> 39.4 us (1.013)
  Pallas kernels: 36.9 us -> 37.4 us
    pallas_call x1, Pallas kernels: 36.9 us -> 37.4 us  [body(): pl.pallas_call(kernel, out_shape=jax.ShapeDtypeStruct((DEP, 256, WIDTH),...]
where the time goes in v6:
time: 39.4 us; the launch traced here: 39.3 us
  Pallas kernels  37.4 us (95%)
  local copies, waits for them, and re-layouts  1.87 us (5%)
    pallas_call x1, Pallas kernels, body(): pl.pallas_call(kernel, out_shape=jax.ShapeDtypeStruct((DEP, 256, WIDTH),...  37.4 us
    unnamed x1, local copies, waits for them, and re-layouts  1.87 us

profile of v6, /device:TPU:1, one launch (start us, length us, event | category | flops | bytes accessed | tf_op | source)
XLA Modules:
  0.0 39.3 jit_solution(9146498556321363388)
XLA Ops:
  0.0 37.4 %encode_decode.1 = bf16[8,256,128]{2,1,0:T(8,128)(2,1)} custom-call(bf16[8,256,128]{2,1,0:T(8,128)(2,1)} %bitcast.9, bf16[16,4,32,512]{3,2,1,0:T(8,128)(2,1)} %bitcast.7, bf16[27,16,512]{2,1,0:T(8,128)(2,1)} %bitcast.10, bf16[16,4,32,512]{3,2,1,0:T(8,128)(2,1)} %bitcast.8, bf16[27,32,32]{2,1,0:T(8,128)(2,1)} %bitcast.11), custom_call_target="tpu_custom_call" | custom-call | tf_op jit(solution)/shard_map/encode_decode/pallas_call | solution.py:477
  37.4 1.9 %copy.7 = bf16[8,32,8,128]{3,2,1,0:T(8,128)(2,1)} copy(bf16[8,32,8,128]{3,2,1,0:T(8,128)(2,1)} %bitcast.6) | data formatting | bytes 1048576

commit v7 on v5

--- a/solution.py
+++ b/solution.py
@@ -194,12 +194,17 @@
             device_id_type=MESH,
         ).start()
 
+    core = col % 2
+
+    def taps_at(ref, start, size):
+        return ref.at[pl.ds(start, size)]
+
     weight_sends = []
     for j in range(1, GROUP):
         to = (lane + j) % GROUP
         copy = pltpu.make_async_remote_copy(
-            src_ref=weight_piece(to),
-            dst_ref=weight_slot(lane),
+            src_ref=taps_at(weight_piece(to), core * 13, 14),
+            dst_ref=taps_at(weight_slot(lane), core * 13, 14),
             send_sem=w_send.at[j - 1],
             recv_sem=w_recv.at[j - 1],
             device_id=device(row - lane + to, col),
@@ -207,6 +212,15 @@
         )
         copy.start()
         weight_sends.append(copy)
+    twin_sends = []
+    for j in range(1, GROUP):
+        slot = taps_at(weight_slot((lane + j) % GROUP), core * 14, 13)
+        twin_sends.append(
+            pltpu.make_async_remote_copy(
+                src_ref=slot, dst_ref=slot, send_sem=w_send.at[GROUP + j - 2], recv_sem=w_recv.at[GROUP + j - 2],
+                device_id=device(row, col + 1 - 2 * core), device_id_type=MESH,
+            )
+        )
 
     sides, ends = ((0, -1), (1, 1)), ((0, -1, 0), (1, 1, DEP - 1))
     feat_moves = [(feat.at[d], feat_in.at[1 - e], dr, 0) for e, dr, d in ends]
@@ -267,6 +281,10 @@
 
     own_weight.wait()
     for copy in weight_sends:
+        copy.wait()
+    for copy in twin_sends:
+        copy.start()
+    for copy in twin_sends:
         copy.wait()
 
     def patches(heights, start):

time: 38.9 us -> 39.2 us (level); the launches traced: 38.8 us -> 38.7 us
  no operation moved by 1% of the time
where the time goes in v7:
time: 39.2 us; the launch traced here: 38.7 us
  Pallas kernels  36.8 us (94%)
  local copies, waits for them, and re-layouts  1.87 us (5%)
    pallas_call x1, Pallas kernels, body(): pl.pallas_call(kernel, out_shape=jax.ShapeDtypeStruct((DEP, 256, WIDTH),...  36.8 us
    unnamed x1, local copies, waits for them, and re-layouts  1.87 us

profile of v7, /device:TPU:1, one launch (start us, length us, event | category | flops | bytes accessed | tf_op | source)
XLA Modules:
  0.0 38.7 jit_solution(18174580677068750676)
XLA Ops:
  0.0 36.8 %encode_decode.1 = bf16[8,256,128]{2,1,0:T(8,128)(2,1)} custom-call(bf16[8,256,128]{2,1,0:T(8,128)(2,1)} %bitcast.9, bf16[16,4,32,512]{3,2,1,0:T(8,128)(2,1)} %bitcast.7, bf16[27,16,512]{2,1,0:T(8,128)(2,1)} %bitcast.10, bf16[16,4,32,512]{3,2,1,0:T(8,128)(2,1)} %bitcast.8, bf16[27,32,32]{2,1,0:T(8,128)(2,1)} %bitcast.11), custom_call_target="tpu_custom_call" | custom-call | tf_op jit(solution)/shard_map/encode_decode/pallas_call | solution.py:493
  36.8 1.9 %copy.7 = bf16[8,32,8,128]{3,2,1,0:T(8,128)(2,1)} copy(bf16[8,32,8,128]{3,2,1,0:T(8,128)(2,1)} %bitcast.6) | data formatting | bytes 1048576

commit v8 on v5

--- a/solution.py
+++ b/solution.py
@@ -194,20 +194,6 @@
             device_id_type=MESH,
         ).start()
 
-    weight_sends = []
-    for j in range(1, GROUP):
-        to = (lane + j) % GROUP
-        copy = pltpu.make_async_remote_copy(
-            src_ref=weight_piece(to),
-            dst_ref=weight_slot(lane),
-            send_sem=w_send.at[j - 1],
-            recv_sem=w_recv.at[j - 1],
-            device_id=device(row - lane + to, col),
-            device_id_type=MESH,
-        )
-        copy.start()
-        weight_sends.append(copy)
-
     sides, ends = ((0, -1), (1, 1)), ((0, -1, 0), (1, 1, DEP - 1))
     feat_moves = [(feat.at[d], feat_in.at[1 - e], dr, 0) for e, dr, d in ends]
     feat_moves += [(feat_rim.at[s], feat_rim_in.at[1 - s, pl.ds(1, DEP)], 0, dc) for s, dc in sides]
@@ -219,6 +205,20 @@
     ]
     for copy in feat_sends:
         copy.start()
+
+    weight_sends = []
+    for j in range(1, GROUP):
+        to = (lane + j) % GROUP
+        copy = pltpu.make_async_remote_copy(
+            src_ref=weight_piece(to),
+            dst_ref=weight_slot(lane),
+            send_sem=w_send.at[j - 1],
+            recv_sem=w_recv.at[j - 1],
+            device_id=device(row - lane + to, col),
+            device_id_type=MESH,
+        )
+        copy.start()
+        weight_sends.append(copy)
 
     tiles[1, 1 + row] = lowered[row // 8]
 

time: 38.9 us -> 38.9 us (level)
  no operation moved by 1% of the time
where the time goes in v8:
time: 38.9 us; the launch traced here: 38.8 us
  Pallas kernels  36.9 us (95%)
  local copies, waits for them, and re-layouts  1.87 us (5%)
    pallas_call x1, Pallas kernels, body(): pl.pallas_call(kernel, out_shape=jax.ShapeDtypeStruct((DEP, 256, WIDTH),...  36.9 us
    unnamed x1, local copies, waits for them, and re-layouts  1.87 us

profile of v8, /device:TPU:1, one launch (start us, length us, event | category | flops | bytes accessed | tf_op | source)
XLA Modules:
  0.0 38.8 jit_solution(17943275548866723541)
XLA Ops:
  0.0 36.9 %encode_decode.1 = bf16[8,256,128]{2,1,0:T(8,128)(2,1)} custom-call(bf16[8,256,128]{2,1,0:T(8,128)(2,1)} %bitcast.9, bf16[16,4,32,512]{3,2,1,0:T(8,128)(2,1)} %bitcast.7, bf16[27,16,512]{2,1,0:T(8,128)(2,1)} %bitcast.10, bf16[16,4,32,512]{3,2,1,0:T(8,128)(2,1)} %bitcast.8, bf16[27,32,32]{2,1,0:T(8,128)(2,1)} %bitcast.11), custom_call_target="tpu_custom_call" | custom-call | tf_op jit(solution)/shard_map/encode_decode/pallas_call | solution.py:475
  36.9 1.9 %copy.7 = bf16[8,32,8,128]{3,2,1,0:T(8,128)(2,1)} copy(bf16[8,32,8,128]{3,2,1,0:T(8,128)(2,1)} %bitcast.6) | data formatting | bytes 1048576
